TPU v7x, 768 devices: a whole 4x8x12 slice. The times are simulated.
768 devices in a mesh: fsdp: 12 (over z), blk: 64 (over x, y, core).
Axes of the slice: x: 4, y: 8, z: 12, core: 2. Of those that a mesh axis runs over, the one named last changes fastest.
Arguments:
- grads: bfloat16 [12, 16384, 1024], P('fsdp', 'blk')
- l_codes: int32 [16384, 1024], P('blk'), may hold values from 0 to 15
- l_scales: float32 [16384, 16], P('blk'), may hold values from 0.01 to 0.12
- r_codes: int32 [16384, 1024], P('blk'), may hold values from 0 to 15
- r_scales: float32 [16384, 16], P('blk'), may hold values from 0.01 to 0.12
- l_stats: float32 [16384, 1024], P('blk'), may hold values from -3 to 3
- r_stats: float32 [16384, 1024], P('blk'), may hold values from -3 to 3
Outputs:
- update: bfloat16 [16384, 1024], P('blk')
- l_stats_new: float32 [16384, 1024], P('blk')
- r_stats_new: float32 [16384, 1024], P('blk')
All inputs are finite; a program needn't handle non-finite values.
Results may differ from a plain program's by a relative error of at most 0.024.
Values may be sent and summed in bfloat16 or wider, within the bound.
A program may use at most 32 MiB of HBM per device.

v0:
```python
import jax
import jax.numpy as jnp
from jax import lax
from jax.sharding import PartitionSpec as P

BETA = 0.9
EPSILON = 1e-06


def partner_2(value, axis, stride):
    mask = 2**stride
    pairs = [(source, source ^ mask) for source in range(lax.axis_size(axis))]
    return lax.ppermute(value, axis, pairs)


def dequantize(code_rows, scales):
    group_size = code_rows.shape[1] // scales.shape[1]
    scale_rows = jnp.repeat(scales, group_size, axis=1)
    return ((2.0 * code_rows.astype(jnp.float32) - 15.0) / 15.0 * scale_rows).astype(jnp.bfloat16)


def attach(mine, partner, is_upper, join_dim):
    lower_part = jnp.where(is_upper, partner, mine)
    upper_part = jnp.where(is_upper, mine, partner)
    return jnp.concatenate([lower_part, upper_part], axis=join_dim)


def shards(grads, l_codes, l_scales, r_codes, r_scales, l_stats, r_stats):
    summed = lax.psum(grads[0].astype(jnp.float32).astype(jnp.bfloat16), "fsdp")
    row_count = summed.shape[0]
    block_order = summed.shape[1]
    team_size = block_order // row_count
    team_bits = team_size.bit_length() - 1
    member = lax.axis_index("blk") % team_size
    offset = member * row_count
    right_rows = dequantize(r_codes, r_scales)
    left_rows = dequantize(l_codes, l_scales)
    gathered = jnp.stack([summed, right_rows])
    for step_bit in range(team_bits):
        partner = partner_2(gathered, "blk", step_bit)
        gathered = attach(gathered, partner, member // 2**step_bit % 2 == 1, 1)
    full_grad = gathered[0]
    full_root = gathered[1]
    left_gram = (
        lax.dot_general(
            summed, full_grad, (((1,), (1,)), ((), ())), preferred_element_type=jnp.float32
        )
        / block_order
    )
    columns = lax.dynamic_slice_in_dim(full_grad, offset, row_count, 1)
    right_gram = (
        lax.dot_general(
            columns, full_grad, (((0,), (0,)), ((), ())), preferred_element_type=jnp.float32
        )
        / block_order
    )
    left_new = BETA * l_stats + (1.0 - BETA) * left_gram
    right_new = BETA * r_stats + (1.0 - BETA) * right_gram
    mixed_rows = jnp.dot(left_rows, full_grad, preferred_element_type=jnp.float32).astype(
        jnp.bfloat16
    )
    left_new, right_new, mixed_rows = (left_new, right_new, mixed_rows)
    product = jnp.dot(mixed_rows, full_root, preferred_element_type=jnp.float32)
    squares = jnp.stack(
        [jnp.sum(jnp.square(summed.astype(jnp.float32))), jnp.sum(jnp.square(product))]
    )
    for step_bit in range(team_bits):
        squares = squares + partner_2(squares, "blk", step_bit)
    entries = float(block_order * block_order)
    factor = jnp.sqrt(squares[0] / entries) / jnp.sqrt(squares[1] / entries + EPSILON)
    update = (product * factor).astype(jnp.bfloat16)
    return (update, left_new, right_new)


def solution(mesh):
    return jax.shard_map(
        shards,
        mesh=mesh,
        in_specs=(
            P("fsdp", "blk", None),
            P("blk", None),
            P("blk", None),
            P("blk", None),
            P("blk", None),
            P("blk", None),
            P("blk", None),
        ),
        out_specs=(P("blk", None), P("blk", None), P("blk", None)),
        check_vma=False,
    )
```

profile of v0, /device:TPU:1, one launch (start us, length us, event | category | flops | bytes accessed | tf_op | source)
XLA Modules:
  0.0 230.1 jit_solution(10740846513922741088)
XLA Ops:
  7.2 2.1 copy.18
  9.9 114.4 %all-reduce.2.cloned.1.call-done = bf16[256,1024]{0,1:T(8,128)(2,1)} async-done(((bf16[256,1024]{0,1:T(8,128)(2,1)}), bf16[256,1024]{0,1:T(8,128)(2,1)}) %all-reduce.2.cloned.1.call-update) | async-done | bytes 524304 | tf_op jit(solution)/shard_map/psum | solution.py:29
  125.5 10.2 %collective-permute-start = (bf16[2,256,1024]{1,2,0:T(8,128)(2,1)S(1)}, bf16[2,256,1024]{1,2,0:T(8,128)(2,1)}, u32[]{:S(2)}, u32[]{:S(2)}) collective-permute-start(bf16[2,256,1024]{1,2,0:T(8,128)(2,1)S(1)} %pad_maximum_fusion.2), channel_id=1, source_target_pairs={{0,1},{1,0},{2,3},{3,2},{4,5},{5,4},{6,7},{7,6},{8,9},{9,8},{10,11... | collective-permute-start | bytes 3145736 | tf_op jit(solution)/shard_map/ppermute | solution.py:13
  135.7 2.4 %collective-permute-done = bf16[2,256,1024]{1,2,0:T(8,128)(2,1)} collective-permute-done((bf16[2,256,1024]{1,2,0:T(8,128)(2,1)S(1)}, bf16[2,256,1024]{1,2,0:T(8,128)(2,1)}, u32[]{:S(2)}, u32[]{:S(2)}) %collective-permute-start) | collective-permute-done | bytes 1048608 | tf_op jit(solution)/shard_map/ppermute | solution.py:13
  138.1 1.4 broadcast_select_fusion.3
  139.4 1.5 pad_maximum_fusion.1
  140.9 3.1 %collective-permute-start.1 = (bf16[2,512,1024]{1,2,0:T(8,128)(2,1)}, bf16[2,512,1024]{1,2,0:T(8,128)(2,1)}, u32[]{:S(2)}, u32[]{:S(2)}) collective-permute-start(bf16[2,512,1024]{1,2,0:T(8,128)(2,1)} %pad_maximum_fusion.1), channel_id=1, source_target_pairs={{0,2},{1,3},{2,0},{3,1},{4,6},{5,7},{6,4},{7,5},{8,10},{9,11},{10,... | collective-permute-start | bytes 6291464 | tf_op jit(solution)/shard_map/ppermute | solution.py:13
  144.1 2.5 %copy.17 = s32[256,1024]{0,1:T(8,128)} copy(s32[256,1024]{1,0:T(8,128)} %param.8) | data formatting | bytes 2097152 | tf_op args[1]
  146.6 2.5 %copy.20 = f32[256,1024]{0,1:T(8,128)} copy(f32[256,1024]{1,0:T(8,128)} %param.12) | data formatting | bytes 2097152 | tf_op args[5]
  149.2 2.6 %copy.21 = f32[256,1024]{0,1:T(8,128)} copy(f32[256,1024]{1,0:T(8,128)} %param.13) | data formatting | bytes 2097152 | tf_op args[6]
  151.7 1.4 fusion.30
  154.0 35.9 %collective-permute-done.1 = bf16[2,512,1024]{1,2,0:T(8,128)(2,1)} collective-permute-done((bf16[2,512,1024]{1,2,0:T(8,128)(2,1)}, bf16[2,512,1024]{1,2,0:T(8,128)(2,1)}, u32[]{:S(2)}, u32[]{:S(2)}) %collective-permute-start.1) | collective-permute-done | bytes 2097184 | tf_op jit(solution)/shard_map/ppermute | solution.py:13
  190.0 2.4 %broadcast_select_fusion.1 = (bf16[2,512,1024]{1,2,0:T(8,128)(2,1)S(1)}, bf16[2,512,1024]{1,2,0:T(8,128)(2,1)S(1)}) fusion(bf16[2,512,1024]{1,2,0:T(8,128)(2,1)} %collective-permute-done.1, pred[]{:T(512)S(6)} %eq.10, bf16[2,256,1024]{1,2,0:T(8,128)(2,1)S(1)} %get-tuple-element.12, bf16[2,256,1024]{1,2,0:T(8,128)(2,1)S(1)} %get-tuple-element.11), kind=kLoop, calls=%fused_computation.15 | loop fusion | flops 6291456 | bytes 8388609 | tf_op jit(solution)/shard_map/jit(_where)/select_n | solution.py:23
  192.4 1.3 copy-done
  194.6 4.4 %multiply_reduce_fusion = (f32[]{:T(128)}, f32[256,1024]{1,0:T(8,128)}) fusion(bf16[2,512,1024]{1,2,0:T(8,128)(2,1)} %copy-done.1, bf16[2,512,1024]{1,2,0:T(8,128)(2,1)} %copy-done, bf16[256,1024]{0,1:T(8,128)(2,1)S(1)} %fusion.30, bf16[1,1024,1024]{1,2,0:T(8,128)(2,1)S(1)} %fusion), kind=kOutput, calls=%fused_computation.28 | convolution fusion | flops 1078722560 | bytes 7864324 | tf_op jit(solution)/shard_map/dot_general | solution.py:63
  199.1 1.3 pad_maximum_fusion.3
  200.4 3.1 %collective-permute-start.2 = (f32[2]{0:T(128)S(1)}, f32[2]{0:T(128)S(1)}, u32[]{:S(2)}, u32[]{:S(2)}) collective-permute-start(f32[2]{0:T(128)S(1)} %pad_maximum_fusion.3), channel_id=1, source_target_pairs={{0,1},{1,0},{2,3},{3,2},{4,5},{5,4},{6,7},{7,6},{8,9},{9,8},{10,11... | collective-permute-start | bytes 32 | tf_op jit(solution)/shard_map/ppermute | solution.py:13
  203.5 2.9 %fusion.17 = f32[256,1024]{0,1:T(8,128)} fusion(bf16[256,1024]{0,1:T(8,128)(2,1)S(1)} %copy-done.2, bf16[1,1024,1024]{1,2,0:T(8,128)(2,1)S(1)} %fusion, f32[256,1024]{0,1:T(8,128)} %copy.20), kind=kOutput, calls=%fused_computation.18 | convolution fusion | flops 537657344 | bytes 4718592 | tf_op jit(solution)/shard_map/dot_general | solution.py:45
  206.5 2.6 %copy.23 = f32[256,1024]{1,0:T(8,128)} copy(f32[256,1024]{0,1:T(8,128)} %fusion.17) | data formatting | bytes 2097152
  209.1 1.7 fusion.23
  210.8 2.6 %copy.24 = f32[256,1024]{1,0:T(8,128)} copy(f32[256,1024]{0,1:T(8,128)} %fusion.23) | data formatting | bytes 2097152
  213.4 1.3 fusion.42
  214.8 3.1 %collective-permute-start.3 = (f32[2]{0:T(128)S(1)}, f32[2]{0:T(128)S(1)}, u32[]{:S(2)}, u32[]{:S(2)}) collective-permute-start(f32[2]{0:T(128)S(1)} %fusion.42), channel_id=1, source_target_pairs={{0,2},{1,3},{2,0},{3,1},{4,6},{5,7},{6,4},{7,5},{8,10},{9,11},{10,... | collective-permute-start | bytes 32 | tf_op jit(solution)/shard_map/ppermute | solution.py:13
  219.0 1.3 fusion.43
  (26 shorter events, 6.3 us)
Async XLA Ops:
  7.2 2.2 copy-start.4
  7.2 2.5 %copy-start.6 = (f32[256,16]{0,1:T(8,128)S(1)}, f32[256,16]{0,1:T(8,128)}, u32[]{:S(2)}) copy-start(f32[256,16]{0,1:T(8,128)} %param.11) | copy-start | bytes 49156
  7.2 117.1 %all-reduce.2.cloned.1.call-start = ((), (), s32[]{:S(2)}) async-start(), calls=%async_computation | async-start | bytes 1048576 | tf_op jit(solution)/shard_map/psum | solution.py:29
  124.3 13.8 %copy-start.2 = (bf16[256,1024]{0,1:T(8,128)(2,1)S(1)}, bf16[256,1024]{0,1:T(8,128)(2,1)}, u32[]{:S(2)}) copy-start(bf16[256,1024]{0,1:T(8,128)(2,1)} %all-reduce.2.cloned.1.call-done) | copy-start | bytes 1572868
  125.5 12.6 %collective-permute-start = (bf16[2,256,1024]{1,2,0:T(8,128)(2,1)S(1)}, bf16[2,256,1024]{1,2,0:T(8,128)(2,1)}, u32[]{:S(2)}, u32[]{:S(2)}) collective-permute-start(bf16[2,256,1024]{1,2,0:T(8,128)(2,1)S(1)} %pad_maximum_fusion.2), channel_id=1, source_target_pairs={{0,1},{1,0},{2,3},{3,2},{4,5},{5,4},{6,7},{7,6},{8,9},{9,8},{10,11... | collective-permute-start | bytes 3145736 | tf_op jit(solution)/shard_map/ppermute | solution.py:13
  140.9 49.0 %collective-permute-start.1 = (bf16[2,512,1024]{1,2,0:T(8,128)(2,1)}, bf16[2,512,1024]{1,2,0:T(8,128)(2,1)}, u32[]{:S(2)}, u32[]{:S(2)}) collective-permute-start(bf16[2,512,1024]{1,2,0:T(8,128)(2,1)} %pad_maximum_fusion.1), channel_id=1, source_target_pairs={{0,2},{1,3},{2,0},{3,1},{4,6},{5,7},{6,4},{7,5},{8,10},{9,11},{10,... | collective-permute-start | bytes 6291464 | tf_op jit(solution)/shard_map/ppermute | solution.py:13
  146.6 5.1 %copy-start.7 = (f32[256,16]{0,1:T(8,128)S(1)}, f32[256,16]{0,1:T(8,128)}, u32[]{:S(2)}) copy-start(f32[256,16]{0,1:T(8,128)} %param.9) | copy-start | bytes 49156
  192.4 1.3 copy-start
  192.4 2.0 copy-start.1
  200.4 13.0 %collective-permute-start.2 = (f32[2]{0:T(128)S(1)}, f32[2]{0:T(128)S(1)}, u32[]{:S(2)}, u32[]{:S(2)}) collective-permute-start(f32[2]{0:T(128)S(1)} %pad_maximum_fusion.3), channel_id=1, source_target_pairs={{0,1},{1,0},{2,3},{3,2},{4,5},{5,4},{6,7},{7,6},{8,9},{9,8},{10,11... | collective-permute-start | bytes 32 | tf_op jit(solution)/shard_map/ppermute | solution.py:13
  206.4 2.6 %copy-start.3 = (f32[256,1024]{0,1:T(8,128)S(1)}, f32[256,1024]{0,1:T(8,128)}, u32[]{:S(2)}) copy-start(f32[256,1024]{0,1:T(8,128)} %copy.21) | copy-start | bytes 3145732
  210.8 11.5 %copy-start.5 = (f32[256,1024]{1,0:T(8,128)S(1)}, f32[256,1024]{1,0:T(8,128)}, u32[]{:S(2)}) copy-start(f32[256,1024]{1,0:T(8,128)} %get-tuple-element.16) | copy-start | bytes 3145732
  214.8 4.3 %collective-permute-start.3 = (f32[2]{0:T(128)S(1)}, f32[2]{0:T(128)S(1)}, u32[]{:S(2)}, u32[]{:S(2)}) collective-permute-start(f32[2]{0:T(128)S(1)} %fusion.42), channel_id=1, source_target_pairs={{0,2},{1,3},{2,0},{3,1},{4,6},{5,7},{6,4},{7,5},{8,10},{9,11},{10,... | collective-permute-start | bytes 32 | tf_op jit(solution)/shard_map/ppermute | solution.py:13
Sparse Core Ops, SparseCore 0:
  10.9 113.3 all-reduce.1
where the time goes:
time: 231 us; the launch traced here: 230 us
  waiting for transfers between devices  154 us (67%)
  starting transfers between devices  19.5 us (8%)
  local copies, waits for them, and re-layouts  17.9 us (8%)
  between operations  15.6 us (7%)
  other arithmetic  14.2 us (6%)
  matrix products  9.09 us (4%)
    psum x1, waiting for transfers between devices, shards(): summed = lax.psum(grads[0].astype(jnp.float32).astype(jnp.bfloat16), 'fsdp')  114 us
    ppermute x4, waiting for transfers between devices, partner_2(): return lax.ppermute(value, axis, pairs)  39.5 us
    ppermute x4, starting transfers between devices, partner_2(): return lax.ppermute(value, axis, pairs)  19.5 us
    unnamed x23, local copies, waits for them, and re-layouts  17.3 us
  transfers between devices with their start and end apart: 5, of which 4 were waited for; matrix products, arithmetic and copies ran while one was open for 9% of the time, Pallas kernels for 0%

commit v1 on v0

v1 whole, which is shorter than its diff:
```python
import functools

import jax
import jax.numpy as jnp
from jax import lax
from jax.experimental import pallas as pl
from jax.experimental.pallas import tpu as pltpu
from jax.sharding import PartitionSpec as P

BETA = 0.9
EPSILON = 1e-06
MESH = pl.DeviceIdType.MESH
F32 = jnp.float32
BF16 = jnp.bfloat16

ROWS = 256
ORDER = 1024
TEAM = 4
RING = 12
LANES = 128
CHUNK = 176
GROUP = 3 * CHUNK
PANEL_ROWS = RING * CHUNK
PAIRS = 4

KEYS = (-5, -4, -3, -2, -1, 1, 2, 3, 4, 5, 6)
SLOT = {key: at for at, key in enumerate(KEYS)}
SLOT[0] = 11
RS = {name: at for at, name in enumerate(
    [("a", 1), ("a", -1), ("b", 1), ("c", 1), ("c", -1), ("d", 1), ("d", -1),
     ("e", 1), ("e", -1), ("f", 1), ("f", -1)])}


def panel_row(pair, half):
    return pair * GROUP + half * ROWS


def kernel(grads, l_codes, l_scales, r_codes, r_scales, l_stats, r_stats,
           update, l_out, r_out,
           x, acc, rbuf, gall, l_code_v, r_code_v, l_scale_v, r_scale_v, l_stat_v, r_stat_v,
           l_root, r_all, mixed, prod, upd_v, sq,
           load_sem, rs_send, rs_recv, ag_send, ag_recv, y_send, y_recv, c_send, c_recv,
           r_send, r_recv, s_send, s_recv, out_sem):
    z = lax.axis_index("fsdp")
    blk = lax.axis_index("blk")
    member = lax.rem(blk, TEAM)
    base = blk - member
    m_y = lax.rem(member + 2, TEAM)
    m_c = member + 1 - 2 * lax.rem(member, 2)
    m_yc = lax.rem(m_c + 2, TEAM)

    def ring(step):
        return (lax.rem(z + step + RING, RING), blk)

    def mate(which):
        return (z, base + which)

    grad_loads = []
    for panel in range(2 * PAIRS):
        grad_loads.append(pltpu.make_async_copy(
            grads.at[0, :, pl.ds(panel * LANES, LANES)],
            x.at[pl.ds(panel_row(panel // 2, panel % 2), ROWS)], load_sem.at[panel]))
    other = [
        pltpu.make_async_copy(r_scales, r_scale_v, load_sem.at[8]),
        pltpu.make_async_copy(r_codes, r_code_v, load_sem.at[9]),
        pltpu.make_async_copy(l_scales, l_scale_v, load_sem.at[10]),
        pltpu.make_async_copy(l_codes, l_code_v, load_sem.at[11]),
        pltpu.make_async_copy(l_stats, l_stat_v, load_sem.at[12]),
        pltpu.make_async_copy(r_stats, r_stat_v, load_sem.at[13]),
    ]
    for copy in grad_loads + other:
        copy.start()

    barrier = pltpu.get_barrier_semaphore()
    partners = [ring(1), ring(-1), ring(2), ring(-2), mate(m_y), mate(m_c), mate(m_yc)]
    for partner in partners:
        pl.semaphore_signal(barrier, inc=1, device_id=partner, device_id_type=MESH)
    for pair in range(PAIRS):
        x[pl.ds(pair * GROUP + 2 * ROWS, 16), :] = jnp.zeros((16, LANES), BF16)
    pl.semaphore_wait(barrier, len(partners))

    def chunk_at(key):
        owner = lax.rem(z + key + RING, RING)
        return pl.ds(pl.multiple_of(owner * CHUNK, 16), CHUNK)

    def remote(src, dst, send, recv, target):
        return pltpu.make_async_remote_copy(
            src_ref=src, dst_ref=dst, send_sem=send, recv_sem=recv,
            device_id=target, device_id_type=MESH)

    sends = []

    def rs_copy(src, name, step):
        copy = remote(src, rbuf.at[RS[name]], rs_send.at[RS[name]], rs_recv.at[RS[name]], ring(step))
        copy.start()
        sends.append(copy)

    def rs_wait(name):
        at = RS[name]
        remote(rbuf.at[at], rbuf.at[at], rs_send.at[at], rs_recv.at[at], ring(1)).wait_recv()
        return rbuf[at].astype(F32)

    for copy in grad_loads:
        copy.wait()
    rs_copy(x.at[chunk_at(6)], ("b", 1), 2)
    rs_copy(x.at[chunk_at(-5)], ("a", -1), -1)
    rs_copy(x.at[chunk_at(5)], ("a", 1), 1)
    for s in (1, -1):
        rs_copy(x.at[chunk_at(3 * s)], ("c", s), s)
    for s in (1, -1):
        rs_copy(x.at[chunk_at(s)], ("e", s), s)

    spread_group = lax.broadcasted_iota(jnp.int32, (48, ORDER), 0) % 16
    spread_column = lax.broadcasted_iota(jnp.int32, (48, ORDER), 1) // 64
    spread = jnp.where(spread_group == spread_column, 1.0, 0.0).astype(BF16)

    def dequantize(codes, scales):
        scaled = scales[...] * (1.0 / 15.0)
        first = scaled.astype(BF16)
        rest = scaled - first.astype(F32)
        second = rest.astype(BF16)
        third = (rest - second.astype(F32)).astype(BF16)
        terms = jnp.concatenate([first.astype(F32), second.astype(F32), third.astype(F32)], axis=0)
        wide = lax.dot_general(jnp.transpose(terms).astype(BF16), spread, (((1,), (0,)), ((), ())),
                               preferred_element_type=F32)
        return ((2.0 * codes[...].astype(F32) - 15.0) * wide).astype(BF16)

    for copy in other[:2]:
        copy.wait()
    r_all[member] = dequantize(r_code_v, r_scale_v)
    r_y = remote(r_all.at[member], r_all.at[member], r_send.at[0], r_recv.at[0], mate(m_y))
    r_c = remote(r_all.at[member], r_all.at[member], r_send.at[1], r_recv.at[1], mate(m_c))
    r_y.start()
    r_c.start()

    for s in (-1, 1):
        total = x[chunk_at(4 * s), :].astype(F32) + rs_wait(("a", s))
        if s == 1:
            total = total + rs_wait(("b", 1))
        acc[0 if s == 1 else 1] = total.astype(BF16)
        rs_copy(acc.at[0 if s == 1 else 1], ("d", s), 2 * s)
    for copy in other[2:4]:
        copy.wait()
    l_root[...] = dequantize(l_code_v, l_scale_v)
    for s in (-1, 1):
        total = x[chunk_at(2 * s), :].astype(F32) + rs_wait(("c", s)) + rs_wait(("d", s))
        acc[2 if s == 1 else 3] = total.astype(BF16)
        rs_copy(acc.at[2 if s == 1 else 3], ("f", s), 2 * s)
    total = x[chunk_at(0), :].astype(F32)
    for s in (-1, 1):
        total = total + rs_wait(("e", s)) + rs_wait(("f", s))
    gall[member, chunk_at(0), :] = total.astype(BF16)

    def z_send(key, step):
        to = key - step
        at = SLOT[6 if to == -6 else to]
        ref = gall.at[member, chunk_at(key)]
        copy = remote(ref, ref, ag_send.at[at], ag_recv.at[at], ring(step))
        copy.start()
        sends.append(copy)

    def z_wait(key):
        ref = gall.at[member, chunk_at(key)]
        at = SLOT[key]
        remote(ref, ref, ag_send.at[at], ag_recv.at[at], ring(1)).wait_recv()

    def y_forward(key):
        ref = gall.at[member, chunk_at(key)]
        at = SLOT[key]
        copy = remote(ref, ref, y_send.at[at], y_recv.at[at], mate(m_y))
        copy.start()
        sends.append(copy)

    def c_forward(key, which, set_at):
        ref = gall.at[which, chunk_at(key)]
        at = SLOT[key] + 12 * set_at
        copy = remote(ref, ref, c_send.at[at], c_recv.at[at], mate(m_c))
        copy.start()
        sends.append(copy)

    def y_wait(key):
        ref = gall.at[m_y, chunk_at(key)]
        at = SLOT[key]
        remote(ref, ref, y_send.at[at], y_recv.at[at], mate(m_y)).wait_recv()
        c_forward(key, m_y, 1)

    def c_wait(key, which, set_at):
        ref = gall.at[which, chunk_at(key)]
        at = SLOT[key] + 12 * set_at
        remote(ref, ref, c_send.at[at], c_recv.at[at], mate(m_c)).wait_recv()

    for s in (1, -1):
        z_send(0, 2 * s)
    for s in (1, -1):
        z_send(0, s)
    y_forward(0)
    c_forward(0, member, 0)
    remote(r_all.at[m_y], r_all.at[m_y], r_send.at[0], r_recv.at[0], mate(m_y)).wait_recv()
    r_yc = remote(r_all.at[m_y], r_all.at[m_y], r_send.at[2], r_recv.at[2], mate(m_c))
    r_yc.start()
    for s in (1, -1):
        z_wait(-2 * s)
        z_send(-2 * s, 2 * s)
        z_send(-2 * s, s)
        y_forward(-2 * s)
        c_forward(-2 * s, member, 0)
    for s in (1, -1):
        z_wait(-s)
        y_forward(-s)
        c_forward(-s, member, 0)
    y_wait(0)
    for s in (1, -1):
        z_wait(-4 * s)
        if s == 1:
            z_send(-4, 2)
        z_send(-4 * s, s)
        y_forward(-4 * s)
        c_forward(-4 * s, member, 0)
    for s in (1, -1):
        z_wait(-3 * s)
        y_forward(-3 * s)
        c_forward(-3 * s, member, 0)
    for key in (-2, 2, -1, 1):
        y_wait(key)
    for key in (-5, 5, 6):
        z_wait(key)
        y_forward(key)
        c_forward(key, member, 0)
    for key in (-4, 4, -3, 3, -5, 5, 6):
        y_wait(key)
    remote(r_all.at[m_c], r_all.at[m_c], r_send.at[1], r_recv.at[1], mate(m_c)).wait_recv()
    remote(r_all.at[m_yc], r_all.at[m_yc], r_send.at[2], r_recv.at[2], mate(m_c)).wait_recv()
    for key in (0,) + KEYS:
        c_wait(key, m_c, 0)
    for key in (0,) + KEYS:
        c_wait(key, m_yc, 1)

    def columns(pair):
        parts = []
        for which in range(TEAM):
            parts.append(jnp.concatenate(
                [gall[which, pl.ds(panel_row(pair, half), ROWS), :] for half in (0, 1)], axis=1))
        return jnp.concatenate(parts, axis=0)

    def rows_of(which):
        return jnp.concatenate(
            [gall[which, pl.ds(panel_row(panel // 2, panel % 2), ROWS), :]
             for panel in range(2 * PAIRS)], axis=1)

    for pair in range(PAIRS):
        mixed[:, pl.ds(pair * ROWS, ROWS)] = jnp.dot(
            l_root[...], columns(pair), preferred_element_type=F32).astype(BF16)
    square = jnp.zeros((ROWS, ROWS), F32)
    for pair in range(PAIRS):
        right = jnp.concatenate([r_all[which, :, pl.ds(pair * ROWS, ROWS)] for which in range(TEAM)], axis=0)
        part = jnp.dot(mixed[...], right, preferred_element_type=F32)
        prod[:, pl.ds(pair * ROWS, ROWS)] = part
        square = square + part * part
    mine = rows_of(member)
    grad_square = jnp.sum(jnp.square(mine.astype(F32)), axis=0, keepdims=True)
    grad_square = sum(grad_square[:, at * LANES:(at + 1) * LANES] for at in range(8))
    prod_square = jnp.sum(square, axis=0, keepdims=True)
    prod_square = prod_square[:, :LANES] + prod_square[:, LANES:]
    sq[3] = jnp.concatenate(
        [jnp.broadcast_to(grad_square, (8, LANES)), jnp.broadcast_to(prod_square, (8, LANES))], axis=0)
    for at, which in enumerate((m_y, m_c, m_yc)):
        copy = remote(sq.at[3], sq.at[at], s_send.at[at], s_recv.at[at], mate(which))
        copy.start()
        sends.append(copy)

    for copy in other[4:]:
        copy.wait()
    scale = (1.0 - BETA) / ORDER
    for which in range(TEAM):
        cut = pl.ds(which * ROWS, ROWS)
        gram = lax.dot_general(mine, rows_of(which), (((1,), (1,)), ((), ())), preferred_element_type=F32)
        l_stat_v[:, cut] = BETA * l_stat_v[:, cut] + scale * gram
    l_store = pltpu.make_async_copy(l_stat_v, l_out, out_sem.at[0])
    l_store.start()
    own_columns = []
    for which in range(TEAM):
        halves = []
        for half in (0, 1):
            start = pl.multiple_of(member * GROUP + half * ROWS, 16)
            halves.append(gall[which, pl.ds(start, ROWS), :])
        own_columns.append(jnp.transpose(jnp.concatenate(halves, axis=1)))
    own_columns = jnp.concatenate(own_columns, axis=1)
    for pair in range(PAIRS):
        cut = pl.ds(pair * ROWS, ROWS)
        gram = jnp.dot(own_columns, columns(pair), preferred_element_type=F32)
        r_stat_v[:, cut] = BETA * r_stat_v[:, cut] + scale * gram
    r_store = pltpu.make_async_copy(r_stat_v, r_out, out_sem.at[1])
    r_store.start()

    for at in range(3):
        remote(sq.at[at], sq.at[at], s_send.at[at], s_recv.at[at], mate(m_y)).wait_recv()
    both = sq[0] + sq[1] + sq[2] + sq[3]
    entries = float(ORDER * ORDER)
    grad_mean = jnp.sum(both[0:1, :], axis=1, keepdims=True) / entries
    prod_mean = jnp.sum(both[8:9, :], axis=1, keepdims=True) / entries
    factor = jnp.sqrt(grad_mean) / jnp.sqrt(prod_mean + EPSILON)
    upd_v[...] = (prod[...] * factor).astype(BF16)
    u_store = pltpu.make_async_copy(upd_v, update, out_sem.at[2])
    u_store.start()
    for copy in sends + [r_y, r_c, r_yc]:
        copy.wait_send()
    l_store.wait()
    r_store.wait()
    u_store.wait()


def shards(grads, l_codes, l_scales, r_codes, r_scales, l_stats, r_stats):
    any_spec = pl.BlockSpec(memory_space=pl.ANY)
    wide = (ROWS, ORDER)
    dma = pltpu.SemaphoreType.DMA
    return pl.pallas_call(
        kernel,
        name="shampoo",
        out_shape=(
            jax.ShapeDtypeStruct(wide, BF16),
            jax.ShapeDtypeStruct(wide, F32),
            jax.ShapeDtypeStruct(wide, F32),
        ),
        in_specs=[any_spec] * 7,
        out_specs=(any_spec,) * 3,
        scratch_shapes=[
            pltpu.VMEM((PANEL_ROWS, LANES), BF16),
            pltpu.VMEM((4, CHUNK, LANES), BF16),
            pltpu.VMEM((11, CHUNK, LANES), BF16),
            pltpu.VMEM((TEAM, PANEL_ROWS, LANES), BF16),
            pltpu.VMEM(wide, jnp.int32),
            pltpu.VMEM(wide, jnp.int32),
            pltpu.VMEM((16, ROWS), F32),
            pltpu.VMEM((16, ROWS), F32),
            pltpu.VMEM(wide, F32),
            pltpu.VMEM(wide, F32),
            pltpu.VMEM(wide, BF16),
            pltpu.VMEM((TEAM, ROWS, ORDER), BF16),
            pltpu.VMEM(wide, BF16),
            pltpu.VMEM(wide, F32),
            pltpu.VMEM(wide, BF16),
            pltpu.VMEM((4, 16, LANES), F32),
            dma((14,)), dma((11,)), dma((11,)), dma((12,)), dma((12,)), dma((12,)), dma((12,)),
            dma((24,)), dma((24,)), dma((3,)), dma((3,)), dma((3,)), dma((3,)), dma((3,)),
        ],
        compiler_params=pltpu.CompilerParams(
            collective_id=0, has_side_effects=True, vmem_limit_bytes=63 * 2**20),
    )(grads, l_codes, l_scales.T, r_codes, r_scales.T, l_stats, r_stats)


def solution(mesh):
    return jax.shard_map(
        shards,
        mesh=mesh,
        in_specs=(
            P("fsdp", "blk", None),
            P("blk", None),
            P("blk", None),
            P("blk", None),
            P("blk", None),
            P("blk", None),
            P("blk", None),
        ),
        out_specs=(P("blk", None), P("blk", None), P("blk", None)),
        check_vma=False,
    )
```

time: 231 us -> 57.4 us (0.25)
  waiting for transfers between devices: 154 us -> 0 us
  Pallas kernels: 0 us -> 52 us
  starting transfers between devices: 19.5 us -> 0 us
  between operations: 15.6 us -> 0.65 us
  other arithmetic: 14.2 us -> 0 us
  local copies, waits for them, and re-layouts: 17.9 us -> 4.53 us
  matrix products: 9.09 us -> 0 us
    psum x1 -> x0, waiting for transfers between devices: 114 us -> none  [shards(): summed = lax.psum(grads[0].astype(jnp.float32).astype(jnp.bfloat16), 'fsdp')]
    pallas_call x0 -> x1, Pallas kernels: none -> 52 us  [shards(): pl.pallas_call(kernel, name='shampoo', out_shape=(jax.ShapeDtypeStruct(wi...]
    ppermute x4 -> x0, waiting for transfers between devices: 39.5 us -> none  [partner_2(): return lax.ppermute(value, axis, pairs)]
    ppermute x4 -> x0, starting transfers between devices: 19.5 us -> none  [partner_2(): return lax.ppermute(value, axis, pairs)]
    unnamed x23 -> x7, local copies, waits for them, and re-layouts: 17.3 us -> 4.53 us
    dot_general x3 -> x0, matrix products: 9.09 us -> none  [the longest x1 4.42 us: shards(): product = jnp.dot(mixed_rows, full_root, preferred_element_type=jnp.float32)]
    select_n x2 -> x0, other arithmetic: 3.73 us -> none  [attach(): lower_part = jnp.where(is_upper, partner, mine)]
    add x2 -> x0, other arithmetic: 2.69 us -> none  [shards(): squares = squares + partner_2(squares, 'blk', step_bit)]
  transfers between devices with their start and end apart: 5 -> 0, of which waited for: 4 -> 0; matrix products, arithmetic and copies ran while one was open for 9% -> 0% of each run, Pallas kernels for 0% -> 0%
where the time goes in v1:
time: 57.4 us; the launch traced here: 57.2 us
  Pallas kernels  52 us (91%)
  local copies, waits for them, and re-layouts  4.53 us (8%)
  between operations  0.65 us (1%)
    pallas_call x1, Pallas kernels, shards(): pl.pallas_call(kernel, name='shampoo', out_shape=(jax.ShapeDtypeStruct(wi...  52 us
    unnamed x7, local copies, waits for them, and re-layouts  4.53 us

profile of v1, /device:TPU:1, one launch (start us, length us, event | category | flops | bytes accessed | tf_op | source)
XLA Modules:
  0.0 57.2 jit_solution(15872667535820461696)
XLA Ops:
  0.6 52.0 %shampoo.1 = (bf16[256,1024]{1,0:T(8,128)(2,1)}, f32[256,1024]{1,0:T(8,128)}, f32[256,1024]{1,0:T(8,128)}) custom-call(bf16[1,256,1024]{2,1,0:T(8,128)(2,1)} %grads.1, s32[256,1024]{1,0:T(8,128)} %l_codes.1, f32[16,256]{1,0:T(8,128)} %bitcast.2, s32[256,1024]{1,0:T(8,128)} %r_codes.1, f32[16,256]{1,0:T(8,128)} %bitcast.3, f32[256,1024]{1,0:T(8,128)} %l_stats.1, ...), custom_call_target="tpu_custom_call" | custom-call | tf_op jit(solution)/shard_map/shampoo/pallas_call | solution.py:316
  52.6 0.0 copy-start.1
  52.6 2.0 %copy.13 = bf16[256,1024]{1,0:T(8,128)(2,1)} copy(bf16[256,1024]{1,0:T(8,128)(2,1)} %get-tuple-element.6) | data formatting | bytes 1048576
  54.6 0.0 copy-done.1
  54.6 0.0 copy-start
  54.6 1.0 %copy.14 = f32[256,1024]{1,0:T(8,128)} copy(f32[256,1024]{1,0:T(8,128)S(1)} %copy-done.1) | data formatting | bytes 2097152
  55.6 0.6 %copy-done = f32[256,1024]{1,0:T(8,128)S(1)} copy-done((f32[256,1024]{1,0:T(8,128)S(1)}, f32[256,1024]{1,0:T(8,128)}, u32[]{:S(2)}) %copy-start) | copy-done | bytes 1048600
  56.2 1.0 %copy.15 = f32[256,1024]{1,0:T(8,128)} copy(f32[256,1024]{1,0:T(8,128)S(1)} %copy-done) | data formatting | bytes 2097152
Async XLA Ops:
  52.6 2.0 %copy-start.1 = (f32[256,1024]{1,0:T(8,128)S(1)}, f32[256,1024]{1,0:T(8,128)}, u32[]{:S(2)}) copy-start(f32[256,1024]{1,0:T(8,128)} %get-tuple-element.7) | copy-start | bytes 3145732
  54.6 1.6 %copy-start = (f32[256,1024]{1,0:T(8,128)S(1)}, f32[256,1024]{1,0:T(8,128)}, u32[]{:S(2)}) copy-start(f32[256,1024]{1,0:T(8,128)} %get-tuple-element.8) | copy-start | bytes 3145732

commit v2 on v1

v2 whole, which is shorter than its diff:
```python
import functools

import jax
import jax.numpy as jnp
from jax import lax
from jax.experimental import pallas as pl
from jax.experimental.pallas import tpu as pltpu
from jax.sharding import PartitionSpec as P

BETA = 0.9
EPSILON = 1e-06
MESH = pl.DeviceIdType.MESH
F32 = jnp.float32
BF16 = jnp.bfloat16

ROWS = 256
ORDER = 1024
TEAM = 4
RING = 12
LANES = 128
CHUNK = 176
GROUP = 3 * CHUNK
PAIRS = 4

KEYS = (0, -3, 3, -1, 1, -4, 4, -2, 2, -5, 5, 6)
SLOT = {key: at for at, key in enumerate(KEYS)}
LEAVES = (("far", 1), ("two", 1), ("two", -1), ("one", 1), ("one", -1), ("back", 1), ("back", -1))
RS = {name: at for at, name in enumerate(
    LEAVES + (("near", 1), ("near", -1), ("node", 1), ("node", -1)))}
PIECES = ((0, 96), (96, 80))


def kernel(grads, l_codes, l_scales, r_codes, r_scales, l_stats, r_stats,
           update, l_out, r_out,
           x, acc, rbuf, gall, l_code_v, r_code_v, l_scale_v, r_scale_v,
           l_root, r_all, mixed, prod, sq,
           load_sem, rs_send, rs_recv, ag_send, ag_recv, y_send, y_recv, c_send, c_recv,
           r_send, r_recv, s_send, s_recv):
    z = lax.axis_index("fsdp")
    blk = lax.axis_index("blk")
    member = lax.rem(blk, TEAM)
    base = blk - member
    m_y = lax.rem(member + 2, TEAM)
    m_c = member + 1 - 2 * lax.rem(member, 2)
    m_yc = lax.rem(m_c + 2, TEAM)

    def ring(step):
        return (lax.rem(z + step + RING, RING), blk)

    def mate(which):
        return (z, base + which)

    grad_loads = []
    for pair in range(PAIRS):
        for panel, row, rows, chunk, at in (
                (0, 0, 176, 0, 0), (0, 176, 80, 1, 0), (1, 0, 96, 1, 80), (1, 96, 160, 2, 0)):
            grad_loads.append(pltpu.make_async_copy(
                grads.at[0, pl.ds(row, rows), pl.ds((2 * pair + panel) * LANES, LANES)],
                x.at[3 * pair + chunk, pl.ds(at, rows)], load_sem.at[len(grad_loads)]))
    other = [
        pltpu.make_async_copy(r_scales, r_scale_v, load_sem.at[16]),
        pltpu.make_async_copy(r_codes, r_code_v, load_sem.at[17]),
        pltpu.make_async_copy(l_scales, l_scale_v, load_sem.at[18]),
        pltpu.make_async_copy(l_codes, l_code_v, load_sem.at[19]),
        pltpu.make_async_copy(l_stats, l_out, load_sem.at[20]),
        pltpu.make_async_copy(r_stats, r_out, load_sem.at[21]),
    ]
    for copy in grad_loads + other:
        copy.start()

    barrier = pltpu.get_barrier_semaphore()
    partners = [ring(step) for step in (3, -3, 2, -2, 1, -1)] + [mate(m_y), mate(m_c), mate(m_yc)]
    for partner in partners:
        pl.semaphore_signal(barrier, inc=1, device_id=partner, device_id_type=MESH)
    for pair in range(PAIRS):
        x[3 * pair + 2, pl.ds(160, 16), :] = jnp.zeros((16, LANES), BF16)
    pl.semaphore_wait(barrier, len(partners))

    def owner(key):
        return lax.rem(z + key + RING, RING)

    def remote(src, dst, send, recv, target):
        return pltpu.make_async_remote_copy(
            src_ref=src, dst_ref=dst, send_sem=send, recv_sem=recv,
            device_id=target, device_id_type=MESH)

    sends = []

    def rs_copy(src, name, piece, step):
        at = piece * 11 + RS[name]
        cut = pl.ds(*PIECES[piece])
        copy = remote(src, rbuf.at[RS[name], cut], rs_send.at[at], rs_recv.at[at], ring(step))
        copy.start()
        sends.append(copy)

    def rs_wait(name, piece):
        at = piece * 11 + RS[name]
        ref = rbuf.at[RS[name], pl.ds(*PIECES[piece])]
        remote(ref, ref, rs_send.at[at], rs_recv.at[at], ring(1)).wait_recv()
        return ref[...].astype(F32)

    def turn(piece):
        return 1 if piece % 2 == 0 else -1

    for copy in grad_loads:
        copy.wait()
    for piece in range(len(PIECES)):
        cut = pl.ds(*PIECES[piece])
        s = turn(piece)
        rs_copy(x.at[owner(6), cut], ("far", 1), piece, 3 * s)
        for s in (1, -1):
            rs_copy(x.at[owner(5 * s), cut], ("two", s), piece, 2 * s)
        for s in (1, -1):
            rs_copy(x.at[owner(4 * s), cut], ("one", s), piece, s)
        for s in (1, -1):
            rs_copy(x.at[owner(2 * s), cut], ("back", s), piece, -s)

    spread_group = lax.broadcasted_iota(jnp.int32, (48, ORDER), 0) % 16
    spread_column = lax.broadcasted_iota(jnp.int32, (48, ORDER), 1) // 64
    spread = jnp.where(spread_group == spread_column, 1.0, 0.0).astype(BF16)

    def dequantize(codes, scales):
        scaled = scales[...] * (1.0 / 15.0)
        first = scaled.astype(BF16)
        rest = scaled - first.astype(F32)
        second = rest.astype(BF16)
        third = (rest - second.astype(F32)).astype(BF16)
        terms = jnp.concatenate([first.astype(F32), second.astype(F32), third.astype(F32)], axis=0)
        wide = lax.dot_general(jnp.transpose(terms).astype(BF16), spread, (((1,), (0,)), ((), ())),
                               preferred_element_type=F32)
        return ((2.0 * codes[...].astype(F32) - 15.0) * wide).astype(BF16)

    for copy in other[:2]:
        copy.wait()
    r_all[member] = dequantize(r_code_v, r_scale_v)
    r_y = remote(r_all.at[member], r_all.at[member], r_send.at[0], r_recv.at[0], mate(m_y))
    r_c = remote(r_all.at[member], r_all.at[member], r_send.at[1], r_recv.at[1], mate(m_c))
    r_y.start()
    r_c.start()

    for piece in range(len(PIECES)):
        cut = pl.ds(*PIECES[piece])
        for s in (-turn(piece), turn(piece)):
            total = x[owner(3 * s), cut, :].astype(F32)
            for name in ("one", "back", "two"):
                total = total + rs_wait((name, s), piece)
            if s == turn(piece):
                total = total + rs_wait(("far", 1), piece)
            at = 0 if s == 1 else 1
            acc[at, cut, :] = total.astype(BF16)
            rs_copy(acc.at[at, cut], ("node", s), piece, 3 * s)
        for s in (1, -1):
            rs_copy(x.at[owner(s), cut], ("near", s), piece, s)
    for copy in other[2:4]:
        copy.wait()
    l_root[...] = dequantize(l_code_v, l_scale_v)

    def z_send(key, piece, step):
        to = key - step
        at = piece * 12 + SLOT[6 if to == -6 else to]
        ref = gall.at[member, owner(key), pl.ds(*PIECES[piece])]
        copy = remote(ref, ref, ag_send.at[at], ag_recv.at[at], ring(step))
        copy.start()
        sends.append(copy)

    def z_wait(key, piece):
        at = piece * 12 + SLOT[key]
        ref = gall.at[member, owner(key), pl.ds(*PIECES[piece])]
        remote(ref, ref, ag_send.at[at], ag_recv.at[at], ring(1)).wait_recv()

    def y_forward(key, piece):
        at = piece * 12 + SLOT[key]
        ref = gall.at[member, owner(key), pl.ds(*PIECES[piece])]
        copy = remote(ref, ref, y_send.at[at], y_recv.at[at], mate(m_y))
        copy.start()
        sends.append(copy)

    def y_wait(key, piece):
        at = piece * 12 + SLOT[key]
        ref = gall.at[m_y, owner(key), pl.ds(*PIECES[piece])]
        remote(ref, ref, y_send.at[at], y_recv.at[at], mate(m_y)).wait_recv()

    def c_copy(which, piece, set_at):
        at = piece * 2 + set_at
        ref = gall.at[which, :, pl.ds(*PIECES[piece])]
        return remote(ref, ref, c_send.at[at], c_recv.at[at], mate(m_c))

    def c_forward(which, piece, set_at):
        copy = c_copy(which, piece, set_at)
        copy.start()
        sends.append(copy)

    for piece in range(len(PIECES)):
        cut = pl.ds(*PIECES[piece])
        total = x[z, cut, :].astype(F32)
        for name in ("near", "node"):
            for s in (-turn(piece), turn(piece)):
                total = total + rs_wait((name, s), piece)
        gall[member, z, cut, :] = total.astype(BF16)
        for s in (turn(piece), -turn(piece)):
            z_send(0, piece, 3 * s)
        for s in (1, -1):
            z_send(0, piece, s)
        y_forward(0, piece)
    for piece in range(len(PIECES)):
        for s in (turn(piece), -turn(piece)):
            z_wait(-3 * s, piece)
            if s == turn(piece):
                z_send(-3 * s, piece, 3 * s)
            z_send(-3 * s, piece, 2 * s)
            z_send(-3 * s, piece, s)
            z_send(-3 * s, piece, -s)
            y_forward(-3 * s, piece)
        for s in (1, -1):
            z_wait(-s, piece)
            y_forward(-s, piece)
    remote(r_all.at[m_y], r_all.at[m_y], r_send.at[0], r_recv.at[0], mate(m_y)).wait_recv()
    r_yc = remote(r_all.at[m_y], r_all.at[m_y], r_send.at[2], r_recv.at[2], mate(m_c))
    r_yc.start()
    for piece in range(len(PIECES)):
        for key in KEYS[5:]:
            z_wait(key, piece)
            y_forward(key, piece)
        c_forward(member, piece, 0)
    for piece in range(len(PIECES)):
        for key in KEYS:
            y_wait(key, piece)
        c_forward(m_y, piece, 1)
    remote(r_all.at[m_c], r_all.at[m_c], r_send.at[1], r_recv.at[1], mate(m_c)).wait_recv()
    remote(r_all.at[m_yc], r_all.at[m_yc], r_send.at[2], r_recv.at[2], mate(m_c)).wait_recv()
    for piece in range(len(PIECES)):
        c_copy(m_c, piece, 0).wait_recv()
        c_copy(m_yc, piece, 1).wait_recv()

    def panel_pair(which, pair):
        both = gall[which, pl.ds(3 * pair, 3)].reshape(GROUP, LANES)
        return jnp.concatenate([both[:ROWS], both[ROWS:2 * ROWS]], axis=1)

    def columns(pair):
        parts = []
        for which in range(TEAM):
            parts.append(panel_pair(which, pair))
        return jnp.concatenate(parts, axis=0)

    def rows_of(which):
        return jnp.concatenate([panel_pair(which, pair) for pair in range(PAIRS)], axis=1)

    for pair in range(PAIRS):
        mixed[:, pl.ds(pair * ROWS, ROWS)] = jnp.dot(
            l_root[...], columns(pair), preferred_element_type=F32).astype(BF16)
    square = jnp.zeros((ROWS, ROWS), F32)
    for pair in range(PAIRS):
        right = jnp.concatenate([r_all[which, :, pl.ds(pair * ROWS, ROWS)] for which in range(TEAM)], axis=0)
        part = jnp.dot(mixed[...], right, preferred_element_type=F32)
        prod[:, pl.ds(pair * ROWS, ROWS)] = part
        square = square + part * part
    mine = rows_of(member)
    grad_square = jnp.sum(jnp.square(mine.astype(F32)), axis=0, keepdims=True)
    grad_square = sum(grad_square[:, at * LANES:(at + 1) * LANES] for at in range(8))
    prod_square = jnp.sum(square, axis=0, keepdims=True)
    prod_square = prod_square[:, :LANES] + prod_square[:, LANES:]
    sq[3] = jnp.concatenate(
        [jnp.broadcast_to(grad_square, (8, LANES)), jnp.broadcast_to(prod_square, (8, LANES))], axis=0)
    for at, which in enumerate((m_y, m_c, m_yc)):
        copy = remote(sq.at[3], sq.at[at], s_send.at[at], s_recv.at[at], mate(which))
        copy.start()
        sends.append(copy)

    for copy in other[4:]:
        copy.wait()
    scale = (1.0 - BETA) / ORDER
    for which in range(TEAM):
        cut = pl.ds(which * ROWS, ROWS)
        gram = lax.dot_general(mine, rows_of(which), (((1,), (1,)), ((), ())), preferred_element_type=F32)
        l_out[:, cut] = BETA * l_out[:, cut] + scale * gram
    own_columns = []
    for which in range(TEAM):
        own_columns.append(jnp.transpose(panel_pair(which, member)))
    own_columns = jnp.concatenate(own_columns, axis=1)
    for pair in range(PAIRS):
        cut = pl.ds(pair * ROWS, ROWS)
        gram = jnp.dot(own_columns, columns(pair), preferred_element_type=F32)
        r_out[:, cut] = BETA * r_out[:, cut] + scale * gram

    for at in range(3):
        remote(sq.at[at], sq.at[at], s_send.at[at], s_recv.at[at], mate(m_y)).wait_recv()
    both = sq[0] + sq[1] + sq[2] + sq[3]
    entries = float(ORDER * ORDER)
    grad_mean = jnp.sum(both[0:1, :], axis=1, keepdims=True) / entries
    prod_mean = jnp.sum(both[8:9, :], axis=1, keepdims=True) / entries
    factor = jnp.sqrt(grad_mean) / jnp.sqrt(prod_mean + EPSILON)
    update[...] = (prod[...] * factor).astype(BF16)
    for copy in sends + [r_y, r_c, r_yc]:
        copy.wait_send()


def store_kernel(a, b, c, a_out, b_out, c_out, sem):
    copies = []
    for src, dst in ((b, b_out), (c, c_out), (a, a_out)):
        for part in range(4):
            cut = pl.ds(part * 64, 64)
            copies.append(pltpu.make_async_copy(src.at[cut], dst.at[cut], sem.at[len(copies)]))
    for copy in copies:
        copy.start()
    for copy in copies:
        copy.wait()


def shards(grads, l_codes, l_scales, r_codes, r_scales, l_stats, r_stats):
    any_spec = pl.BlockSpec(memory_space=pl.ANY)
    wide = (ROWS, ORDER)
    dma = pltpu.SemaphoreType.DMA
    pieces = len(PIECES)
    outs = pl.pallas_call(
        kernel,
        name="shampoo",
        out_shape=(
            pltpu.VMEM(wide, BF16),
            pltpu.VMEM(wide, F32),
            pltpu.VMEM(wide, F32),
        ),
        in_specs=[any_spec] * 7,
        out_specs=(pl.BlockSpec(memory_space=pltpu.VMEM),) * 3,
        scratch_shapes=[
            pltpu.VMEM((RING, CHUNK, LANES), BF16),
            pltpu.VMEM((2, CHUNK, LANES), BF16),
            pltpu.VMEM((11, CHUNK, LANES), BF16),
            pltpu.VMEM((TEAM, RING, CHUNK, LANES), BF16),
            pltpu.VMEM(wide, jnp.int32),
            pltpu.VMEM(wide, jnp.int32),
            pltpu.VMEM((16, ROWS), F32),
            pltpu.VMEM((16, ROWS), F32),
            pltpu.VMEM(wide, BF16),
            pltpu.VMEM((TEAM, ROWS, ORDER), BF16),
            pltpu.VMEM(wide, BF16),
            pltpu.VMEM(wide, F32),
            pltpu.VMEM((4, 16, LANES), F32),
            dma((22,)), dma((11 * pieces,)), dma((11 * pieces,)), dma((12 * pieces,)), dma((12 * pieces,)),
            dma((12 * pieces,)), dma((12 * pieces,)), dma((2 * pieces,)), dma((2 * pieces,)),
            dma((3,)), dma((3,)), dma((3,)), dma((3,)),
        ],
        compiler_params=pltpu.CompilerParams(
            collective_id=0, has_side_effects=True, vmem_limit_bytes=40 * 2**20),
    )(*[pltpu.with_memory_space_constraint(a, pltpu.HBM) for a in (grads, l_codes, l_scales.T, r_codes, r_scales.T, l_stats, r_stats)])
    return pl.pallas_call(
        store_kernel,
        name="store",
        out_shape=(pltpu.HBM(wide, BF16), pltpu.HBM(wide, F32), pltpu.HBM(wide, F32)),
        in_specs=[any_spec] * 3,
        out_specs=(any_spec,) * 3,
        scratch_shapes=[dma((12,))],
        compiler_params=pltpu.CompilerParams(vmem_limit_bytes=16 * 2**20),
    )(*outs)


def solution(mesh):
    return jax.shard_map(
        shards,
        mesh=mesh,
        in_specs=(
            P("fsdp", "blk", None),
            P("blk", None),
            P("blk", None),
            P("blk", None),
            P("blk", None),
            P("blk", None),
            P("blk", None),
        ),
        out_specs=(P("blk", None), P("blk", None), P("blk", None)),
        check_vma=False,
    )
```

time: 57.4 us -> 52 us (0.906)
  local copies, waits for them, and re-layouts: 4.53 us -> 0 us
  Pallas kernels: 52 us -> 51.2 us
    unnamed x7 -> x0, local copies, waits for them, and re-layouts: 4.53 us -> none
    pallas_call x1 -> x2, Pallas kernels: 52 us -> 51.2 us  [the longest x1 49.6 us: shards(): pl.pallas_call(kernel, name='shampoo', out_shape=(pltpu.VMEM(wide, BF16),...]
where the time goes in v2:
time: 52 us; the launch traced here: 51.9 us
  Pallas kernels  51.2 us (98%)
  between operations  0.64 us (1%)
    pallas_call x1, Pallas kernels, shards(): pl.pallas_call(kernel, name='shampoo', out_shape=(pltpu.VMEM(wide, BF16),...  49.6 us
    pallas_call x1, Pallas kernels, shards(): pl.pallas_call(store_kernel, name='store', out_shape=(pltpu.HBM(wide, BF1...  1.58 us

profile of v2, /device:TPU:1, one launch (start us, length us, event | category | flops | bytes accessed | tf_op | source)
XLA Modules:
  0.0 51.9 jit_solution(17399111022107190025)
XLA Ops:
  0.6 49.6 %shampoo.1 = (bf16[256,1024]{1,0:T(8,128)(2,1)S(1)}, f32[256,1024]{1,0:T(8,128)S(1)}, f32[256,1024]{1,0:T(8,128)S(1)}) custom-call(bf16[1,256,1024]{2,1,0:T(8,128)(2,1)} %grads.1, s32[256,1024]{1,0:T(8,128)} %l_codes.1, f32[16,256]{1,0:T(8,128)} %bitcast.2, s32[256,1024]{1,0:T(8,128)} %r_codes.1, f32[16,256]{1,0:T(8,128)} %bitcast.3, f32[256,1024]{1,0:T(8,128)} %l_stats.1, ...), custom_call_target="tpu_custom_call" | custom-call | tf_op jit(solution)/shard_map/shampoo/pallas_call | solution.py:314
  50.3 1.6 %store.1 = (bf16[256,1024]{1,0:T(8,128)(2,1)}, f32[256,1024]{1,0:T(8,128)}, f32[256,1024]{1,0:T(8,128)}) custom-call(bf16[256,1024]{1,0:T(8,128)(2,1)S(1)} %get-tuple-element.6.a, f32[256,1024]{1,0:T(8,128)S(1)} %get-tuple-element.7.b, f32[256,1024]{1,0:T(8,128)S(1)} %get-tuple-element.8.c), custom_call_target="tpu_custom_call" | custom-call | tf_op jit(solution)/shard_map/store/pallas_call | solution.py:345

commit v3 on v2

v3 whole, which is shorter than its diff:
```python
import functools

import jax
import jax.numpy as jnp
from jax import lax
from jax.experimental import pallas as pl
from jax.experimental.pallas import tpu as pltpu
from jax.sharding import PartitionSpec as P

BETA = 0.9
EPSILON = 1e-06
MESH = pl.DeviceIdType.MESH
F32 = jnp.float32
BF16 = jnp.bfloat16

ROWS = 256
ORDER = 1024
TEAM = 4
RING = 12
LANES = 128
CHUNK = 176
GROUP = 3 * CHUNK
PAIRS = 4

KEYS = (0, -3, 3, -1, 1, -4, 4, -2, 2, -5, 5, 6)
SLOT = {key: at for at, key in enumerate(KEYS)}
PIECES = ((0, 96), (96, 80))
DIAGONAL = (3, 5, 6)
LINKS = {1: (0, 1), 2: (1, 1), 4: (0, 4), 3: (4, -1), 5: (4, 1), 6: (4, 2)}


def tree(turn):
    links = {}
    for far, (near, step) in LINKS.items():
        if far == 6:
            links[6] = (-turn * near, turn * step)
        else:
            for s in (turn, -turn):
                links[-s * far] = (-s * near, s * step)
    return links


def depth(links, key):
    return 0 if key == 0 else 1 + depth(links, links[key][0])


def height(links, key):
    return max([1 + height(links, far) for far, (near, _) in links.items() if near == key], default=0)


def turn_of(piece):
    return 1 if piece % 2 == 0 else -1


def kernel(grads, l_codes, l_scales, r_codes, r_scales, l_stats, r_stats,
           update, l_out, r_out,
           x, acc, rbuf, gall, l_code_v, r_code_v, l_scale_v, r_scale_v,
           l_root, r_all, total, mixed, prod, sq,
           load_sem, rs_send, rs_recv, ag_send, ag_recv, y_send, y_recv, c_send, c_recv,
           r_send, r_recv, s_send, s_recv):
    z = lax.axis_index("fsdp")
    blk = lax.axis_index("blk")
    member = lax.rem(blk, TEAM)
    base = blk - member
    m_y = lax.rem(member + 2, TEAM)
    m_c = member + 1 - 2 * lax.rem(member, 2)
    m_yc = lax.rem(m_c + 2, TEAM)

    def ring(step, which=None):
        return (lax.rem(z + step + RING, RING), blk if which is None else base + which)

    def mate(which):
        return (z, base + which)

    barrier = pltpu.get_barrier_semaphore()
    steps = sorted({abs(step) for _, step in LINKS.values()})
    partners = [ring(s * step) for step in steps for s in (1, -1)] + [mate(m_y), mate(m_c), mate(m_yc)]
    cross = sorted({abs(LINKS[key][1]) for key in DIAGONAL})
    partners += [ring(s * step, m_y) for step in cross for s in (1, -1)]
    for partner in partners:
        pl.semaphore_signal(barrier, inc=1, device_id=partner, device_id_type=MESH)

    grad_loads = []
    for pair in range(PAIRS):
        for panel, row, rows, chunk, at in (
                (0, 0, 176, 0, 0), (0, 176, 80, 1, 0), (1, 0, 96, 1, 80), (1, 96, 160, 2, 0)):
            grad_loads.append(pltpu.make_async_copy(
                grads.at[0, pl.ds(row, rows), pl.ds((2 * pair + panel) * LANES, LANES)],
                x.at[3 * pair + chunk, pl.ds(at, rows)], load_sem.at[len(grad_loads)]))
    other = [
        pltpu.make_async_copy(r_scales, r_scale_v, load_sem.at[16]),
        pltpu.make_async_copy(r_codes, r_code_v, load_sem.at[17]),
        pltpu.make_async_copy(l_scales, l_scale_v, load_sem.at[18]),
        pltpu.make_async_copy(l_codes, l_code_v, load_sem.at[19]),
        pltpu.make_async_copy(l_stats, l_out, load_sem.at[20]),
        pltpu.make_async_copy(r_stats, r_out, load_sem.at[21]),
    ]
    for copy in grad_loads + other:
        copy.start()

    for pair in range(PAIRS):
        x[3 * pair + 2, pl.ds(160, 16), :] = jnp.zeros((16, LANES), BF16)
    pl.semaphore_wait(barrier, len(partners))

    def owner(key):
        return lax.rem(z + key + RING, RING)

    def remote(src, dst, send, recv, target):
        return pltpu.make_async_remote_copy(
            src_ref=src, dst_ref=dst, send_sem=send, recv_sem=recv,
            device_id=target, device_id_type=MESH)

    sends = []

    def rs_copy(src, key, piece):
        step = tree(turn_of(piece))[key][1]
        at = piece * 12 + SLOT[key]
        copy = remote(src, rbuf.at[SLOT[key], pl.ds(*PIECES[piece])], rs_send.at[at], rs_recv.at[at], ring(-step))
        copy.start()
        sends.append(copy)

    def rs_wait(key, piece):
        at = piece * 12 + SLOT[key]
        ref = rbuf.at[SLOT[key], pl.ds(*PIECES[piece])]
        remote(ref, ref, rs_send.at[at], rs_recv.at[at], ring(1)).wait_recv()
        return ref[...].astype(F32)

    def gathered(key, piece):
        links = tree(turn_of(piece))
        total = x[owner(key), pl.ds(*PIECES[piece]), :].astype(F32)
        beyond = [far for far in links if links[far][0] == key]
        for far in sorted(beyond, key=lambda far: height(links, far)):
            total = total + rs_wait(far, piece)
        return total.astype(BF16)

    for copy in grad_loads:
        copy.wait()
    for piece in range(len(PIECES)):
        links = tree(turn_of(piece))
        leaves = [key for key in links if height(links, key) == 0]
        for key in sorted(leaves, key=lambda key: (-depth(links, key), -abs(links[key][1]))):
            rs_copy(x.at[owner(key), pl.ds(*PIECES[piece])], key, piece)

    spread_group = lax.broadcasted_iota(jnp.int32, (48, ORDER), 0) % 16
    spread_column = lax.broadcasted_iota(jnp.int32, (48, ORDER), 1) // 64
    spread = jnp.where(spread_group == spread_column, 1.0, 0.0).astype(BF16)

    def dequantize(codes, scales):
        scaled = scales[...] * (1.0 / 15.0)
        first = scaled.astype(BF16)
        rest = scaled - first.astype(F32)
        second = rest.astype(BF16)
        third = (rest - second.astype(F32)).astype(BF16)
        terms = jnp.concatenate([first.astype(F32), second.astype(F32), third.astype(F32)], axis=0)
        wide = lax.dot_general(jnp.transpose(terms).astype(BF16), spread, (((1,), (0,)), ((), ())),
                               preferred_element_type=F32)
        return ((2.0 * codes[...].astype(F32) - 15.0) * wide).astype(BF16)

    for copy in other[:2]:
        copy.wait()
    r_all[member] = dequantize(r_code_v, r_scale_v)
    r_y = remote(r_all.at[member], r_all.at[member], r_send.at[0], r_recv.at[0], mate(m_y))
    r_c = remote(r_all.at[member], r_all.at[member], r_send.at[1], r_recv.at[1], mate(m_c))
    r_y.start()
    r_c.start()

    links = tree(1)
    for level in range(max(depth(links, key) for key in links), 0, -1):
        for piece in range(len(PIECES)):
            links = tree(turn_of(piece))
            nodes = [key for key in links if height(links, key) and depth(links, key) == level]
            for key in reversed(nodes):
                at = 6 * (level - 1) + nodes.index(key)
                cut = pl.ds(*PIECES[piece])
                acc[at, cut, :] = gathered(key, piece)
                rs_copy(acc.at[at, cut], key, piece)
        if level == 1:
            for copy in other[2:4]:
                copy.wait()
            left = dequantize(l_code_v, l_scale_v)
            for which in range(TEAM):
                l_root[which] = left[:, which * ROWS:(which + 1) * ROWS]

    def z_send(key, piece):
        links = tree(turn_of(piece))
        beyond = [far for far in links if links[far][0] == key]
        ref = gall.at[member, owner(key), pl.ds(*PIECES[piece])]
        for far in sorted(beyond, key=lambda far: (-height(links, far), abs(links[far][1]) * (1 if key else -1))):
            at = piece * 12 + SLOT[far]
            step = links[far][1]
            copies = [remote(ref, ref, ag_send.at[at], ag_recv.at[at], ring(step))]
            if abs(far) in DIAGONAL:
                copies.append(remote(ref, ref, y_send.at[at], y_recv.at[at], ring(step, m_y)))
            for copy in copies:
                copy.start()
                sends.append(copy)

    def z_wait(key, piece):
        at = piece * 12 + SLOT[key]
        ref = gall.at[member, owner(key), pl.ds(*PIECES[piece])]
        remote(ref, ref, ag_send.at[at], ag_recv.at[at], ring(1)).wait_recv()

    def y_forward(key, piece):
        if abs(key) in DIAGONAL:
            return
        at = piece * 12 + SLOT[key]
        ref = gall.at[member, owner(key), pl.ds(*PIECES[piece])]
        copy = remote(ref, ref, y_send.at[at], y_recv.at[at], mate(m_y))
        copy.start()
        sends.append(copy)

    def y_wait(key, piece):
        at = piece * 12 + SLOT[key]
        ref = gall.at[m_y, owner(key), pl.ds(*PIECES[piece])]
        remote(ref, ref, y_send.at[at], y_recv.at[at], mate(m_y)).wait_recv()

    def c_copy(which, piece, set_at):
        at = piece * 2 + set_at
        ref = gall.at[which, :, pl.ds(*PIECES[piece])]
        return remote(ref, ref, c_send.at[at], c_recv.at[at], mate(m_c))

    def c_forward(which, piece, set_at):
        copy = c_copy(which, piece, set_at)
        copy.start()
        sends.append(copy)

    for piece in range(len(PIECES)):
        gall[member, z, pl.ds(*PIECES[piece]), :] = gathered(0, piece)
        z_send(0, piece)
        y_forward(0, piece)
    links = tree(1)
    levels = max(depth(links, key) for key in links)
    for level in range(1, levels + 1):
        for piece in range(len(PIECES)):
            links = tree(turn_of(piece))
            for key in sorted([key for key in links if depth(links, key) == level],
                              key=lambda key: (-height(links, key), abs(links[key][1]))):
                z_wait(key, piece)
                z_send(key, piece)
                y_forward(key, piece)
            if level == levels:
                c_forward(member, piece, 0)
        if level == 1:
            remote(r_all.at[m_y], r_all.at[m_y], r_send.at[0], r_recv.at[0], mate(m_y)).wait_recv()
            r_yc = remote(r_all.at[m_y], r_all.at[m_y], r_send.at[2], r_recv.at[2], mate(m_c))
            r_yc.start()
    for piece in range(len(PIECES)):
        links = tree(turn_of(piece))
        for key in sorted(KEYS, key=lambda key: depth(links, key)):
            y_wait(key, piece)
        c_forward(m_y, piece, 1)
    def panel_pair(which, pair):
        both = gall[which, pl.ds(3 * pair, 3)].reshape(GROUP, LANES)
        return jnp.concatenate([both[:ROWS], both[ROWS:2 * ROWS]], axis=1)

    def rows_of(which):
        return jnp.concatenate([panel_pair(which, pair) for pair in range(PAIRS)], axis=1)

    def mix(which, first=False):
        part = jnp.dot(l_root[which], rows_of(which), preferred_element_type=F32)
        return part if first else total[...] + part

    scale = (1.0 - BETA) / ORDER

    def grams(which, first=False):
        cut = pl.ds(pl.multiple_of(which * ROWS, ROWS), ROWS)
        left = lax.dot_general(rows_of(member), rows_of(which), (((1,), (1,)), ((), ())), preferred_element_type=F32)
        l_out[:, cut] = BETA * l_out[:, cut] + scale * left
        right = jnp.dot(jnp.transpose(panel_pair(which, member)), rows_of(which), preferred_element_type=F32)
        r_out[...] = (BETA * r_out[...] if first else r_out[...]) + scale * right

    total[...] = mix(member, True)
    total[...] = mix(m_y)
    grad_square = jnp.sum(jnp.square(rows_of(member).astype(F32)), axis=0, keepdims=True)
    grad_square = sum(grad_square[:, at * LANES:(at + 1) * LANES] for at in range(8))
    for copy in other[4:]:
        copy.wait()
    grams(member, True)
    remote(r_all.at[m_c], r_all.at[m_c], r_send.at[1], r_recv.at[1], mate(m_c)).wait_recv()
    remote(r_all.at[m_yc], r_all.at[m_yc], r_send.at[2], r_recv.at[2], mate(m_c)).wait_recv()
    for piece in range(len(PIECES)):
        c_copy(m_c, piece, 0).wait_recv()
    total[...] = mix(m_c)
    for piece in range(len(PIECES)):
        c_copy(m_yc, piece, 1).wait_recv()
    mixed[...] = mix(m_yc).astype(BF16)
    square = jnp.zeros((ROWS, ROWS), F32)
    for pair in range(PAIRS):
        right = jnp.concatenate([r_all[which, :, pl.ds(pair * ROWS, ROWS)] for which in range(TEAM)], axis=0)
        part = jnp.dot(mixed[...], right, preferred_element_type=F32)
        prod[:, pl.ds(pair * ROWS, ROWS)] = part
        square = square + part * part
    prod_square = jnp.sum(square, axis=0, keepdims=True)
    prod_square = prod_square[:, :LANES] + prod_square[:, LANES:]
    sq[3] = jnp.concatenate(
        [jnp.broadcast_to(grad_square, (8, LANES)), jnp.broadcast_to(prod_square, (8, LANES))], axis=0)
    for at, which in enumerate((m_y, m_c, m_yc)):
        copy = remote(sq.at[3], sq.at[at], s_send.at[at], s_recv.at[at], mate(which))
        copy.start()
        sends.append(copy)
    for which in (m_y, m_c, m_yc):
        grams(which)

    for at in range(3):
        remote(sq.at[at], sq.at[at], s_send.at[at], s_recv.at[at], mate(m_y)).wait_recv()
    both = sq[0] + sq[1] + sq[2] + sq[3]
    entries = float(ORDER * ORDER)
    grad_mean = jnp.sum(both[0:1, :], axis=1, keepdims=True) / entries
    prod_mean = jnp.sum(both[8:9, :], axis=1, keepdims=True) / entries
    factor = jnp.sqrt(grad_mean) / jnp.sqrt(prod_mean + EPSILON)
    update[...] = (prod[...] * factor).astype(BF16)
    for copy in sends + [r_y, r_c, r_yc]:
        copy.wait_send()


def store_kernel(a, b, c, a_out, b_out, c_out, sem):
    copies = []
    for src, dst in ((b, b_out), (c, c_out), (a, a_out)):
        for part in range(4):
            cut = pl.ds(part * 64, 64)
            copies.append(pltpu.make_async_copy(src.at[cut], dst.at[cut], sem.at[len(copies)]))
    for copy in copies:
        copy.start()
    for copy in copies:
        copy.wait()


def shards(grads, l_codes, l_scales, r_codes, r_scales, l_stats, r_stats):
    any_spec = pl.BlockSpec(memory_space=pl.ANY)
    wide = (ROWS, ORDER)
    dma = pltpu.SemaphoreType.DMA
    pieces = len(PIECES)
    outs = pl.pallas_call(
        kernel,
        name="shampoo",
        out_shape=(
            pltpu.VMEM(wide, BF16),
            pltpu.VMEM(wide, F32),
            pltpu.VMEM(wide, F32),
        ),
        in_specs=[any_spec] * 7,
        out_specs=(pl.BlockSpec(memory_space=pltpu.VMEM),) * 3,
        scratch_shapes=[
            pltpu.VMEM((RING, CHUNK, LANES), BF16),
            pltpu.VMEM((36, CHUNK, LANES), BF16),
            pltpu.VMEM((12, CHUNK, LANES), BF16),
            pltpu.VMEM((TEAM, RING, CHUNK, LANES), BF16),
            pltpu.VMEM(wide, jnp.int32),
            pltpu.VMEM(wide, jnp.int32),
            pltpu.VMEM((16, ROWS), F32),
            pltpu.VMEM((16, ROWS), F32),
            pltpu.VMEM((TEAM, ROWS, ROWS), BF16),
            pltpu.VMEM((TEAM, ROWS, ORDER), BF16),
            pltpu.VMEM(wide, F32),
            pltpu.VMEM(wide, BF16),
            pltpu.VMEM(wide, F32),
            pltpu.VMEM((4, 16, LANES), F32),
            dma((22,)), dma((12 * pieces,)), dma((12 * pieces,)), dma((12 * pieces,)), dma((12 * pieces,)),
            dma((12 * pieces,)), dma((12 * pieces,)), dma((2 * pieces,)), dma((2 * pieces,)),
            dma((3,)), dma((3,)), dma((3,)), dma((3,)),
        ],
        compiler_params=pltpu.CompilerParams(
            collective_id=0, has_side_effects=True, vmem_limit_bytes=40 * 2**20),
    )(*[pltpu.with_memory_space_constraint(a, pltpu.HBM) for a in (grads, l_codes, l_scales.T, r_codes, r_scales.T, l_stats, r_stats)])
    return pl.pallas_call(
        store_kernel,
        name="store",
        out_shape=(pltpu.HBM(wide, BF16), pltpu.HBM(wide, F32), pltpu.HBM(wide, F32)),
        in_specs=[any_spec] * 3,
        out_specs=(any_spec,) * 3,
        scratch_shapes=[dma((12,))],
        compiler_params=pltpu.CompilerParams(vmem_limit_bytes=16 * 2**20),
    )(*outs)


def solution(mesh):
    return jax.shard_map(
        shards,
        mesh=mesh,
        in_specs=(
            P("fsdp", "blk", None),
            P("blk", None),
            P("blk", None),
            P("blk", None),
            P("blk", None),
            P("blk", None),
            P("blk", None),
        ),
        out_specs=(P("blk", None), P("blk", None), P("blk", None)),
        check_vma=False,
    )
```

time: 52 us -> 50.5 us (0.971)
  Pallas kernels: 51.2 us -> 49.7 us
    pallas_call x1, Pallas kernels: 49.6 us -> 48.2 us  [shards(): pl.pallas_call(kernel, name='shampoo', out_shape=(pltpu.VMEM(wide, BF16),...]
where the time goes in v3:
time: 50.5 us; the launch traced here: 50.4 us
  Pallas kernels  49.7 us (98%)
  between operations  0.64 us (1%)
    pallas_call x1, Pallas kernels, shards(): pl.pallas_call(kernel, name='shampoo', out_shape=(pltpu.VMEM(wide, BF16),...  48.2 us
    pallas_call x1, Pallas kernels, shards(): pl.pallas_call(store_kernel, name='store', out_shape=(pltpu.HBM(wide, BF1...  1.58 us

profile of v3, /device:TPU:1, one launch (start us, length us, event | category | flops | bytes accessed | tf_op | source)
XLA Modules:
  0.0 50.4 jit_solution(8208457777261115599)
XLA Ops:
  0.6 48.2 %shampoo.1 = (bf16[256,1024]{1,0:T(8,128)(2,1)S(1)}, f32[256,1024]{1,0:T(8,128)S(1)}, f32[256,1024]{1,0:T(8,128)S(1)}) custom-call(bf16[1,256,1024]{2,1,0:T(8,128)(2,1)} %grads.1, s32[256,1024]{1,0:T(8,128)} %l_codes.1, f32[16,256]{1,0:T(8,128)} %bitcast.2, s32[256,1024]{1,0:T(8,128)} %r_codes.1, f32[16,256]{1,0:T(8,128)} %bitcast.3, f32[256,1024]{1,0:T(8,128)} %l_stats.1, ...), custom_call_target="tpu_custom_call" | custom-call | tf_op jit(solution)/shard_map/shampoo/pallas_call | solution.py:333
  48.8 1.6 %store.1 = (bf16[256,1024]{1,0:T(8,128)(2,1)}, f32[256,1024]{1,0:T(8,128)}, f32[256,1024]{1,0:T(8,128)}) custom-call(bf16[256,1024]{1,0:T(8,128)(2,1)S(1)} %get-tuple-element.6.a, f32[256,1024]{1,0:T(8,128)S(1)} %get-tuple-element.7.b, f32[256,1024]{1,0:T(8,128)S(1)} %get-tuple-element.8.c), custom_call_target="tpu_custom_call" | custom-call | tf_op jit(solution)/shard_map/store/pallas_call | solution.py:365

commit v4 on v3

--- a/solution.py
+++ b/solution.py
@@ -22,9 +22,11 @@
 GROUP = 3 * CHUNK
 PAIRS = 4
 
-KEYS = (0, -3, 3, -1, 1, -4, 4, -2, 2, -5, 5, 6)
-SLOT = {key: at for at, key in enumerate(KEYS)}
-PIECES = ((0, 96), (96, 80))
+KEYS = (0, -3, -5, 6, 5, 3, -1, 1, -4, 4, -2, 2)
+SLOT = {key: at for at, key in enumerate(KEYS[1:])}
+SUM_WAIT = {-4: 0, 4: 1, 0: 2, -1: 3, 1: 4}
+SPREAD_WAIT = {-1: 0, 1: 1, -4: 2, 4: 3, -2: 4, 2: 5, -3: 6, 3: 6, -5: 6, 5: 6, 6: 6}
+PIECES = ((0, 80), (80, 96))
 DIAGONAL = (3, 5, 6)
 LINKS = {1: (0, 1), 2: (1, 1), 4: (0, 4), 3: (4, -1), 5: (4, 1), 6: (4, 2)}
 
@@ -53,9 +55,9 @@
 
 
 def kernel(grads, l_codes, l_scales, r_codes, r_scales, l_stats, r_stats,
-           update, l_out, r_out,
+           prod, l_out, r_out, factor,
            x, acc, rbuf, gall, l_code_v, r_code_v, l_scale_v, r_scale_v,
-           l_root, r_all, total, mixed, prod, sq,
+           l_root, r_all, total, mixed, sq,
            load_sem, rs_send, rs_recv, ag_send, ag_recv, y_send, y_recv, c_send, c_recv,
            r_send, r_recv, s_send, s_recv):
     z = lax.axis_index("fsdp")
@@ -74,7 +76,7 @@
 
     barrier = pltpu.get_barrier_semaphore()
     steps = sorted({abs(step) for _, step in LINKS.values()})
-    partners = [ring(s * step) for step in steps for s in (1, -1)] + [mate(m_y), mate(m_c), mate(m_yc)]
+    partners = [ring(s * step) for step in reversed(steps) for s in (1, -1)] + [mate(m_y), mate(m_c), mate(m_yc)]
     cross = sorted({abs(LINKS[key][1]) for key in DIAGONAL})
     partners += [ring(s * step, m_y) for step in cross for s in (1, -1)]
     for partner in partners:
@@ -113,25 +115,20 @@
     sends = []
 
     def rs_copy(src, key, piece):
-        step = tree(turn_of(piece))[key][1]
-        at = piece * 12 + SLOT[key]
-        copy = remote(src, rbuf.at[SLOT[key], pl.ds(*PIECES[piece])], rs_send.at[at], rs_recv.at[at], ring(-step))
-        copy.start()
-        sends.append(copy)
-
-    def rs_wait(key, piece):
-        at = piece * 12 + SLOT[key]
+        near, step = tree(turn_of(piece))[key]
         ref = rbuf.at[SLOT[key], pl.ds(*PIECES[piece])]
-        remote(ref, ref, rs_send.at[at], rs_recv.at[at], ring(1)).wait_recv()
-        return ref[...].astype(F32)
+        remote(src, ref, rs_send.at[piece], rs_recv.at[5 * piece + SUM_WAIT[near]], ring(-step)).start()
 
     def gathered(key, piece):
         links = tree(turn_of(piece))
-        total = x[owner(key), pl.ds(*PIECES[piece]), :].astype(F32)
-        beyond = [far for far in links if links[far][0] == key]
-        for far in sorted(beyond, key=lambda far: height(links, far)):
-            total = total + rs_wait(far, piece)
-        return total.astype(BF16)
+        cut = pl.ds(*PIECES[piece])
+        slots = sorted(SLOT[far] for far in links if links[far][0] == key)
+        ref = rbuf.at[pl.ds(slots[0], len(slots)), cut]
+        remote(ref, ref, rs_send.at[piece], rs_recv.at[5 * piece + SUM_WAIT[key]], ring(1)).wait_recv()
+        result = x[owner(key), cut, :].astype(F32)
+        for slot in slots:
+            result = result + rbuf[slot, cut, :].astype(F32)
+        return result.astype(BF16)
 
     for copy in grad_loads:
         copy.wait()
@@ -186,33 +183,25 @@
         beyond = [far for far in links if links[far][0] == key]
         ref = gall.at[member, owner(key), pl.ds(*PIECES[piece])]
         for far in sorted(beyond, key=lambda far: (-height(links, far), abs(links[far][1]) * (1 if key else -1))):
-            at = piece * 12 + SLOT[far]
+            at = 7 * piece + SPREAD_WAIT[far]
             step = links[far][1]
-            copies = [remote(ref, ref, ag_send.at[at], ag_recv.at[at], ring(step))]
+            remote(ref, ref, ag_send.at[piece], ag_recv.at[at], ring(step)).start()
             if abs(far) in DIAGONAL:
-                copies.append(remote(ref, ref, y_send.at[at], y_recv.at[at], ring(step, m_y)))
-            for copy in copies:
-                copy.start()
-                sends.append(copy)
+                remote(ref, ref, y_send.at[piece], y_recv.at[piece], ring(step, m_y)).start()
 
     def z_wait(key, piece):
-        at = piece * 12 + SLOT[key]
+        at = 7 * piece + SPREAD_WAIT[key]
+        count = sum(1 for other_key in SPREAD_WAIT if SPREAD_WAIT[other_key] == SPREAD_WAIT[key])
+        ref = gall.at[member, pl.ds(0, count), pl.ds(*PIECES[piece])]
+        remote(ref, ref, ag_send.at[piece], ag_recv.at[at], ring(1)).wait_recv()
+
+    def y_forward(key, piece):
         ref = gall.at[member, owner(key), pl.ds(*PIECES[piece])]
-        remote(ref, ref, ag_send.at[at], ag_recv.at[at], ring(1)).wait_recv()
-
-    def y_forward(key, piece):
-        if abs(key) in DIAGONAL:
-            return
-        at = piece * 12 + SLOT[key]
-        ref = gall.at[member, owner(key), pl.ds(*PIECES[piece])]
-        copy = remote(ref, ref, y_send.at[at], y_recv.at[at], mate(m_y))
-        copy.start()
-        sends.append(copy)
-
-    def y_wait(key, piece):
-        at = piece * 12 + SLOT[key]
-        ref = gall.at[m_y, owner(key), pl.ds(*PIECES[piece])]
-        remote(ref, ref, y_send.at[at], y_recv.at[at], mate(m_y)).wait_recv()
+        remote(ref, ref, y_send.at[piece], y_recv.at[piece], mate(m_y)).start()
+
+    def y_wait(piece):
+        ref = gall.at[m_y, :, pl.ds(*PIECES[piece])]
+        remote(ref, ref, y_send.at[piece], y_recv.at[piece], mate(m_y)).wait_recv()
 
     def c_copy(which, piece, set_at):
         at = piece * 2 + set_at
@@ -233,22 +222,22 @@
     for level in range(1, levels + 1):
         for piece in range(len(PIECES)):
             links = tree(turn_of(piece))
-            for key in sorted([key for key in links if depth(links, key) == level],
-                              key=lambda key: (-height(links, key), abs(links[key][1]))):
+            here = [key for key in links if depth(links, key) == level and abs(key) not in DIAGONAL]
+            for key in sorted(here, key=lambda key: (-height(links, key), abs(links[key][1]))):
                 z_wait(key, piece)
                 z_send(key, piece)
                 y_forward(key, piece)
             if level == levels:
+                z_wait(6, piece)
                 c_forward(member, piece, 0)
         if level == 1:
             remote(r_all.at[m_y], r_all.at[m_y], r_send.at[0], r_recv.at[0], mate(m_y)).wait_recv()
             r_yc = remote(r_all.at[m_y], r_all.at[m_y], r_send.at[2], r_recv.at[2], mate(m_c))
             r_yc.start()
     for piece in range(len(PIECES)):
-        links = tree(turn_of(piece))
-        for key in sorted(KEYS, key=lambda key: depth(links, key)):
-            y_wait(key, piece)
+        y_wait(piece)
         c_forward(m_y, piece, 1)
+
     def panel_pair(which, pair):
         both = gall[which, pl.ds(3 * pair, 3)].reshape(GROUP, LANES)
         return jnp.concatenate([both[:ROWS], both[ROWS:2 * ROWS]], axis=1)
@@ -301,32 +290,44 @@
     for which in (m_y, m_c, m_yc):
         grams(which)
 
+    for copy in sends[:-3] + [r_y, r_c, r_yc]:
+        copy.wait_send()
+    for piece in range(len(PIECES)):
+        cut = pl.ds(*PIECES[piece])
+        ref = rbuf.at[:, cut]
+        remote(ref, ref, rs_send.at[piece], rs_recv.at[5 * piece], ring(1)).wait_send()
+        ref = gall.at[member, pl.ds(0, 11), cut]
+        remote(ref, ref, ag_send.at[piece], ag_recv.at[7 * piece], ring(1)).wait_send()
+        ref = gall.at[member, :, cut]
+        remote(ref, ref, y_send.at[piece], y_recv.at[piece], mate(m_y)).wait_send()
     for at in range(3):
         remote(sq.at[at], sq.at[at], s_send.at[at], s_recv.at[at], mate(m_y)).wait_recv()
     both = sq[0] + sq[1] + sq[2] + sq[3]
     entries = float(ORDER * ORDER)
-    grad_mean = jnp.sum(both[0:1, :], axis=1, keepdims=True) / entries
-    prod_mean = jnp.sum(both[8:9, :], axis=1, keepdims=True) / entries
-    factor = jnp.sqrt(grad_mean) / jnp.sqrt(prod_mean + EPSILON)
-    update[...] = (prod[...] * factor).astype(BF16)
-    for copy in sends + [r_y, r_c, r_yc]:
+    grad_mean = jnp.sum(both[0:8, :], axis=1, keepdims=True) / entries
+    prod_mean = jnp.sum(both[8:16, :], axis=1, keepdims=True) / entries
+    factor[...] = jnp.broadcast_to(jnp.sqrt(grad_mean) / jnp.sqrt(prod_mean + EPSILON), (8, LANES))
+    for copy in sends[-3:]:
         copy.wait_send()
 
 
-def store_kernel(a, b, c, a_out, b_out, c_out, sem):
-    copies = []
-    for src, dst in ((b, b_out), (c, c_out), (a, a_out)):
-        for part in range(4):
-            cut = pl.ds(part * 64, 64)
-            copies.append(pltpu.make_async_copy(src.at[cut], dst.at[cut], sem.at[len(copies)]))
-    for copy in copies:
+def store_kernel(prod, l_new, r_new, factor, update, l_out, r_out, scaled, sem):
+    copies = [
+        pltpu.make_async_copy(l_new, l_out, sem.at[0]),
+        pltpu.make_async_copy(r_new, r_out, sem.at[1]),
+        pltpu.make_async_copy(scaled, update, sem.at[2]),
+    ]
+    for copy in copies[:2]:
         copy.start()
+    scaled[...] = (prod[...] * factor[0:1, 0:1]).astype(BF16)
+    copies[2].start()
     for copy in copies:
         copy.wait()
 
 
 def shards(grads, l_codes, l_scales, r_codes, r_scales, l_stats, r_stats):
     any_spec = pl.BlockSpec(memory_space=pl.ANY)
+    vmem_spec = pl.BlockSpec(memory_space=pltpu.VMEM)
     wide = (ROWS, ORDER)
     dma = pltpu.SemaphoreType.DMA
     pieces = len(PIECES)
@@ -334,16 +335,17 @@
         kernel,
         name="shampoo",
         out_shape=(
-            pltpu.VMEM(wide, BF16),
             pltpu.VMEM(wide, F32),
             pltpu.VMEM(wide, F32),
+            pltpu.VMEM(wide, F32),
+            pltpu.VMEM((8, LANES), F32),
         ),
         in_specs=[any_spec] * 7,
-        out_specs=(pl.BlockSpec(memory_space=pltpu.VMEM),) * 3,
+        out_specs=(vmem_spec,) * 4,
         scratch_shapes=[
             pltpu.VMEM((RING, CHUNK, LANES), BF16),
             pltpu.VMEM((36, CHUNK, LANES), BF16),
-            pltpu.VMEM((12, CHUNK, LANES), BF16),
+            pltpu.VMEM((11, CHUNK, LANES), BF16),
             pltpu.VMEM((TEAM, RING, CHUNK, LANES), BF16),
             pltpu.VMEM(wide, jnp.int32),
             pltpu.VMEM(wide, jnp.int32),
@@ -353,10 +355,9 @@
             pltpu.VMEM((TEAM, ROWS, ORDER), BF16),
             pltpu.VMEM(wide, F32),
             pltpu.VMEM(wide, BF16),
-            pltpu.VMEM(wide, F32),
             pltpu.VMEM((4, 16, LANES), F32),
-            dma((22,)), dma((12 * pieces,)), dma((12 * pieces,)), dma((12 * pieces,)), dma((12 * pieces,)),
-            dma((12 * pieces,)), dma((12 * pieces,)), dma((2 * pieces,)), dma((2 * pieces,)),
+            dma((22,)), dma((pieces,)), dma((5 * pieces,)), dma((pieces,)), dma((7 * pieces,)),
+            dma((pieces,)), dma((pieces,)), dma((2 * pieces,)), dma((2 * pieces,)),
             dma((3,)), dma((3,)), dma((3,)), dma((3,)),
         ],
         compiler_params=pltpu.CompilerParams(
@@ -366,9 +367,9 @@
         store_kernel,
         name="store",
         out_shape=(pltpu.HBM(wide, BF16), pltpu.HBM(wide, F32), pltpu.HBM(wide, F32)),
-        in_specs=[any_spec] * 3,
+        in_specs=[vmem_spec] * 4,
         out_specs=(any_spec,) * 3,
-        scratch_shapes=[dma((12,))],
+        scratch_shapes=[pltpu.VMEM(wide, BF16), dma((3,))],
         compiler_params=pltpu.CompilerParams(vmem_limit_bytes=16 * 2**20),
     )(*outs)
 

time: 50.5 us -> 48.8 us (0.966)
  Pallas kernels: 49.7 us -> 48 us
    pallas_call x1, Pallas kernels: 48.2 us -> 46.5 us  [shards(): pl.pallas_call(kernel, name='shampoo', out_shape=(pltpu.VMEM(wide, F32),...]
where the time goes in v4:
time: 48.8 us; the launch traced here: 48.7 us
  Pallas kernels  48 us (98%)
  between operations  0.64 us (1%)
    pallas_call x1, Pallas kernels, shards(): pl.pallas_call(kernel, name='shampoo', out_shape=(pltpu.VMEM(wide, F32),...  46.5 us
    pallas_call x1, Pallas kernels, shards(): pl.pallas_call(store_kernel, name='store', out_shape=(pltpu.HBM(wide, BF1...  1.51 us

profile of v4, /device:TPU:1, one launch (start us, length us, event | category | flops | bytes accessed | tf_op | source)
XLA Modules:
  0.0 48.7 jit_solution(13211149071585508343)
XLA Ops:
  0.6 46.5 %shampoo.1 = (f32[256,1024]{1,0:T(8,128)S(1)}, f32[256,1024]{1,0:T(8,128)S(1)}, f32[256,1024]{1,0:T(8,128)S(1)}, f32[8,128]{1,0:T(8,128)S(1)}) custom-call(bf16[1,256,1024]{2,1,0:T(8,128)(2,1)} %grads.1, s32[256,1024]{1,0:T(8,128)} %l_codes.1, f32[16,256]{1,0:T(8,128)} %bitcast.2, s32[256,1024]{1,0:T(8,128)} %r_codes.1, f32[16,256]{1,0:T(8,128)} %bitcast.3, ...), custom_call_target="tpu_custom_call" | custom-call | tf_op jit(solution)/shard_map/shampoo/pallas_call | solution.py:334
  47.2 1.5 %store.1 = (bf16[256,1024]{1,0:T(8,128)(2,1)}, f32[256,1024]{1,0:T(8,128)}, f32[256,1024]{1,0:T(8,128)}) custom-call(f32[256,1024]{1,0:T(8,128)S(1)} %get-tuple-element.7.prod, f32[256,1024]{1,0:T(8,128)S(1)} %get-tuple-element.8.l_new, f32[256,1024]{1,0:T(8,128)S(1)} %get-tuple-element.9.r_new, f32[8,128]{1,0:T(8,128)S(1)} %get-tuple-element.10.factor), custom_call_target="tpu_custom_call" | custom-call | tf_op jit(solution)/shard_map/store/pallas_call | solution.py:366

commit v5 on v4

--- a/solution.py
+++ b/solution.py
@@ -25,9 +25,9 @@
 KEYS = (0, -3, -5, 6, 5, 3, -1, 1, -4, 4, -2, 2)
 SLOT = {key: at for at, key in enumerate(KEYS[1:])}
 SUM_WAIT = {-4: 0, 4: 1, 0: 2, -1: 3, 1: 4}
-SPREAD_WAIT = {-1: 0, 1: 1, -4: 2, 4: 3, -2: 4, 2: 5, -3: 6, 3: 6, -5: 6, 5: 6, 6: 6}
+SPREAD_WAIT = {-1: 0, 1: 1, -4: 2, 4: 3, -2: 4, 2: 4, -3: 4, 3: 4, -5: 4, 5: 4, 6: 4}
 PIECES = ((0, 80), (80, 96))
-DIAGONAL = (3, 5, 6)
+DIAGONAL = (2, 3, 5, 6)
 LINKS = {1: (0, 1), 2: (1, 1), 4: (0, 4), 3: (4, -1), 5: (4, 1), 6: (4, 2)}
 
 
@@ -88,14 +88,14 @@
                 (0, 0, 176, 0, 0), (0, 176, 80, 1, 0), (1, 0, 96, 1, 80), (1, 96, 160, 2, 0)):
             grad_loads.append(pltpu.make_async_copy(
                 grads.at[0, pl.ds(row, rows), pl.ds((2 * pair + panel) * LANES, LANES)],
-                x.at[3 * pair + chunk, pl.ds(at, rows)], load_sem.at[len(grad_loads)]))
+                x.at[3 * pair + chunk, pl.ds(at, rows)], load_sem.at[6]))
     other = [
-        pltpu.make_async_copy(r_scales, r_scale_v, load_sem.at[16]),
-        pltpu.make_async_copy(r_codes, r_code_v, load_sem.at[17]),
-        pltpu.make_async_copy(l_scales, l_scale_v, load_sem.at[18]),
-        pltpu.make_async_copy(l_codes, l_code_v, load_sem.at[19]),
-        pltpu.make_async_copy(l_stats, l_out, load_sem.at[20]),
-        pltpu.make_async_copy(r_stats, r_out, load_sem.at[21]),
+        pltpu.make_async_copy(r_scales, r_scale_v, load_sem.at[0]),
+        pltpu.make_async_copy(r_codes, r_code_v, load_sem.at[1]),
+        pltpu.make_async_copy(l_scales, l_scale_v, load_sem.at[2]),
+        pltpu.make_async_copy(l_codes, l_code_v, load_sem.at[3]),
+        pltpu.make_async_copy(l_stats, l_out, load_sem.at[4]),
+        pltpu.make_async_copy(r_stats, r_out, load_sem.at[5]),
     ]
     for copy in grad_loads + other:
         copy.start()
@@ -130,8 +130,7 @@
             result = result + rbuf[slot, cut, :].astype(F32)
         return result.astype(BF16)
 
-    for copy in grad_loads:
-        copy.wait()
+    pltpu.make_async_copy(grads.at[0], mixed, load_sem.at[6]).wait()
     for piece in range(len(PIECES)):
         links = tree(turn_of(piece))
         leaves = [key for key in links if height(links, key) == 0]
@@ -183,14 +182,14 @@
         beyond = [far for far in links if links[far][0] == key]
         ref = gall.at[member, owner(key), pl.ds(*PIECES[piece])]
         for far in sorted(beyond, key=lambda far: (-height(links, far), abs(links[far][1]) * (1 if key else -1))):
-            at = 7 * piece + SPREAD_WAIT[far]
+            at = 5 * piece + SPREAD_WAIT[far]
             step = links[far][1]
             remote(ref, ref, ag_send.at[piece], ag_recv.at[at], ring(step)).start()
             if abs(far) in DIAGONAL:
                 remote(ref, ref, y_send.at[piece], y_recv.at[piece], ring(step, m_y)).start()
 
     def z_wait(key, piece):
-        at = 7 * piece + SPREAD_WAIT[key]
+        at = 5 * piece + SPREAD_WAIT[key]
         count = sum(1 for other_key in SPREAD_WAIT if SPREAD_WAIT[other_key] == SPREAD_WAIT[key])
         ref = gall.at[member, pl.ds(0, count), pl.ds(*PIECES[piece])]
         remote(ref, ref, ag_send.at[piece], ag_recv.at[at], ring(1)).wait_recv()
@@ -262,9 +261,6 @@
     total[...] = mix(m_y)
     grad_square = jnp.sum(jnp.square(rows_of(member).astype(F32)), axis=0, keepdims=True)
     grad_square = sum(grad_square[:, at * LANES:(at + 1) * LANES] for at in range(8))
-    for copy in other[4:]:
-        copy.wait()
-    grams(member, True)
     remote(r_all.at[m_c], r_all.at[m_c], r_send.at[1], r_recv.at[1], mate(m_c)).wait_recv()
     remote(r_all.at[m_yc], r_all.at[m_yc], r_send.at[2], r_recv.at[2], mate(m_c)).wait_recv()
     for piece in range(len(PIECES)):
@@ -284,31 +280,31 @@
     sq[3] = jnp.concatenate(
         [jnp.broadcast_to(grad_square, (8, LANES)), jnp.broadcast_to(prod_square, (8, LANES))], axis=0)
     for at, which in enumerate((m_y, m_c, m_yc)):
-        copy = remote(sq.at[3], sq.at[at], s_send.at[at], s_recv.at[at], mate(which))
-        copy.start()
-        sends.append(copy)
+        remote(sq.at[3], sq.at[at], s_send.at[0], s_recv.at[0], mate(which)).start()
+    for copy in other[4:]:
+        copy.wait()
+    grams(member, True)
     for which in (m_y, m_c, m_yc):
         grams(which)
 
-    for copy in sends[:-3] + [r_y, r_c, r_yc]:
+    for copy in sends + [r_y, r_c, r_yc]:
         copy.wait_send()
     for piece in range(len(PIECES)):
         cut = pl.ds(*PIECES[piece])
         ref = rbuf.at[:, cut]
         remote(ref, ref, rs_send.at[piece], rs_recv.at[5 * piece], ring(1)).wait_send()
         ref = gall.at[member, pl.ds(0, 11), cut]
-        remote(ref, ref, ag_send.at[piece], ag_recv.at[7 * piece], ring(1)).wait_send()
+        remote(ref, ref, ag_send.at[piece], ag_recv.at[5 * piece], ring(1)).wait_send()
         ref = gall.at[member, :, cut]
         remote(ref, ref, y_send.at[piece], y_recv.at[piece], mate(m_y)).wait_send()
-    for at in range(3):
-        remote(sq.at[at], sq.at[at], s_send.at[at], s_recv.at[at], mate(m_y)).wait_recv()
+    squares = remote(sq.at[pl.ds(0, 3)], sq.at[pl.ds(0, 3)], s_send.at[0], s_recv.at[0], mate(m_y))
+    squares.wait_recv()
     both = sq[0] + sq[1] + sq[2] + sq[3]
     entries = float(ORDER * ORDER)
     grad_mean = jnp.sum(both[0:8, :], axis=1, keepdims=True) / entries
     prod_mean = jnp.sum(both[8:16, :], axis=1, keepdims=True) / entries
     factor[...] = jnp.broadcast_to(jnp.sqrt(grad_mean) / jnp.sqrt(prod_mean + EPSILON), (8, LANES))
-    for copy in sends[-3:]:
-        copy.wait_send()
+    squares.wait_send()
 
 
 def store_kernel(prod, l_new, r_new, factor, update, l_out, r_out, scaled, sem):
@@ -356,9 +352,9 @@
             pltpu.VMEM(wide, F32),
             pltpu.VMEM(wide, BF16),
             pltpu.VMEM((4, 16, LANES), F32),
-            dma((22,)), dma((pieces,)), dma((5 * pieces,)), dma((pieces,)), dma((7 * pieces,)),
+            dma((7,)), dma((pieces,)), dma((5 * pieces,)), dma((pieces,)), dma((5 * pieces,)),
             dma((pieces,)), dma((pieces,)), dma((2 * pieces,)), dma((2 * pieces,)),
-            dma((3,)), dma((3,)), dma((3,)), dma((3,)),
+            dma((3,)), dma((3,)), dma((1,)), dma((1,)),
         ],
         compiler_params=pltpu.CompilerParams(
             collective_id=0, has_side_effects=True, vmem_limit_bytes=40 * 2**20),

time: 48.8 us -> 47.9 us (0.982)
  Pallas kernels: 48 us -> 47.1 us
    pallas_call x1, Pallas kernels: 46.5 us -> 45.6 us  [shards(): pl.pallas_call(kernel, name='shampoo', out_shape=(pltpu.VMEM(wide, F32),...]
where the time goes in v5:
time: 47.9 us; the launch traced here: 47.8 us
  Pallas kernels  47.1 us (98%)
  between operations  0.64 us (1%)
    pallas_call x1, Pallas kernels, shards(): pl.pallas_call(kernel, name='shampoo', out_shape=(pltpu.VMEM(wide, F32),...  45.6 us
    pallas_call x1, Pallas kernels, shards(): pl.pallas_call(store_kernel, name='store', out_shape=(pltpu.HBM(wide, BF1...  1.51 us

profile of v5, /device:TPU:1, one launch (start us, length us, event | category | flops | bytes accessed | tf_op | source)
XLA Modules:
  0.0 47.8 jit_solution(9281340432057251974)
XLA Ops:
  0.6 45.6 %shampoo.1 = (f32[256,1024]{1,0:T(8,128)S(1)}, f32[256,1024]{1,0:T(8,128)S(1)}, f32[256,1024]{1,0:T(8,128)S(1)}, f32[8,128]{1,0:T(8,128)S(1)}) custom-call(bf16[1,256,1024]{2,1,0:T(8,128)(2,1)} %grads.1, s32[256,1024]{1,0:T(8,128)} %l_codes.1, f32[16,256]{1,0:T(8,128)} %bitcast.2, s32[256,1024]{1,0:T(8,128)} %r_codes.1, f32[16,256]{1,0:T(8,128)} %bitcast.3, ...), custom_call_target="tpu_custom_call" | custom-call | tf_op jit(solution)/shard_map/shampoo/pallas_call | solution.py:330
  46.2 1.5 %store.1 = (bf16[256,1024]{1,0:T(8,128)(2,1)}, f32[256,1024]{1,0:T(8,128)}, f32[256,1024]{1,0:T(8,128)}) custom-call(f32[256,1024]{1,0:T(8,128)S(1)} %get-tuple-element.7.prod, f32[256,1024]{1,0:T(8,128)S(1)} %get-tuple-element.8.l_new, f32[256,1024]{1,0:T(8,128)S(1)} %get-tuple-element.9.r_new, f32[8,128]{1,0:T(8,128)S(1)} %get-tuple-element.10.factor), custom_call_target="tpu_custom_call" | custom-call | tf_op jit(solution)/shard_map/store/pallas_call | solution.py:362

commit v6 on v5

--- a/solution.py
+++ b/solution.py
@@ -229,13 +229,12 @@
             if level == levels:
                 z_wait(6, piece)
                 c_forward(member, piece, 0)
+                y_wait(piece)
+                c_forward(m_y, piece, 1)
         if level == 1:
             remote(r_all.at[m_y], r_all.at[m_y], r_send.at[0], r_recv.at[0], mate(m_y)).wait_recv()
             r_yc = remote(r_all.at[m_y], r_all.at[m_y], r_send.at[2], r_recv.at[2], mate(m_c))
             r_yc.start()
-    for piece in range(len(PIECES)):
-        y_wait(piece)
-        c_forward(m_y, piece, 1)
 
     def panel_pair(which, pair):
         both = gall[which, pl.ds(3 * pair, 3)].reshape(GROUP, LANES)

time: 47.9 us -> 47.7 us (level)
  no operation moved by 1% of the time
where the time goes in v6:
time: 47.7 us; the launch traced here: 47.5 us
  Pallas kernels  46.9 us (98%)
  between operations  0.64 us (1%)
    pallas_call x1, Pallas kernels, shards(): pl.pallas_call(kernel, name='shampoo', out_shape=(pltpu.VMEM(wide, F32),...  45.4 us
    pallas_call x1, Pallas kernels, shards(): pl.pallas_call(store_kernel, name='store', out_shape=(pltpu.HBM(wide, BF1...  1.51 us

profile of v6, /device:TPU:1, one launch (start us, length us, event | category | flops | bytes accessed | tf_op | source)
XLA Modules:
  0.0 47.5 jit_solution(17561240479283606001)
XLA Ops:
  0.6 45.4 %shampoo.1 = (f32[256,1024]{1,0:T(8,128)S(1)}, f32[256,1024]{1,0:T(8,128)S(1)}, f32[256,1024]{1,0:T(8,128)S(1)}, f32[8,128]{1,0:T(8,128)S(1)}) custom-call(bf16[1,256,1024]{2,1,0:T(8,128)(2,1)} %grads.1, s32[256,1024]{1,0:T(8,128)} %l_codes.1, f32[16,256]{1,0:T(8,128)} %bitcast.2, s32[256,1024]{1,0:T(8,128)} %r_codes.1, f32[16,256]{1,0:T(8,128)} %bitcast.3, ...), custom_call_target="tpu_custom_call" | custom-call | tf_op jit(solution)/shard_map/shampoo/pallas_call | solution.py:329
  46.0 1.5 %store.1 = (bf16[256,1024]{1,0:T(8,128)(2,1)}, f32[256,1024]{1,0:T(8,128)}, f32[256,1024]{1,0:T(8,128)}) custom-call(f32[256,1024]{1,0:T(8,128)S(1)} %get-tuple-element.7.prod, f32[256,1024]{1,0:T(8,128)S(1)} %get-tuple-element.8.l_new, f32[256,1024]{1,0:T(8,128)S(1)} %get-tuple-element.9.r_new, f32[8,128]{1,0:T(8,128)S(1)} %get-tuple-element.10.factor), custom_call_target="tpu_custom_call" | custom-call | tf_op jit(solution)/shard_map/store/pallas_call | solution.py:361
